TPU v7x, 32 devices: a whole 2x2x4 slice. The times are simulated.
32 devices in a mesh: wall: 8 (over y, x, core), stream: 4 (over z).
Axes of the slice: x: 2, y: 2, z: 4, core: 2. Of those that a mesh axis runs over, the one named last changes fastest.
Arguments:
- cotangent: float32 [5, 16, 256, 1024], P(None, None, 'wall', 'stream'), may hold values from -6 to 6
- lower: float32 [5, 256], P(None, 'wall'), may hold values from 0 to 1, as said below
- pivot: float32 [5, 256], P(None, 'wall'), as said below
- speed: float32 [5, 256], P(None, 'wall'), may hold values from 0.5 to 2
Outputs:
- state_grad: float32 [5, 16, 256, 1024], P(None, None, 'wall', 'stream')
Inputs may be any that keep to these rules, and one draw needn't show every extreme that they name: `lower`: every multiplier is strictly between 0 and 1. Every pivot is positive.
All inputs are finite; a program needn't handle non-finite values.
Results may differ from a plain program's by a relative error of at most 0.00012.
Values sent between devices are 32-bit elements; how exact they have to be, the bound alone decides.
A program may use at most 64 MiB of HBM per device.

v0:
```python
import math

import jax
import jax.numpy as jnp
from jax import lax
from jax.sharding import PartitionSpec as P

root_value = (math.sqrt(5.0) - 3.0) / 2.0
inverse_gain = 3.0 / math.sqrt(5.0)
first_coeff = 7.0 / 9.0
second_coeff = 1.0 / 36.0


def prefix(part, axis, combine, identity, reverse):
    count = lax.axis_size(axis)
    place = lax.axis_index(axis)
    ahead = count - 1 - place if reverse else place
    gathered = jax.tree.map(lambda a: lax.all_gather(a, axis), part)
    state = jax.tree.map(lambda a, e: jnp.zeros_like(a) + jnp.asarray(e, a.dtype), part, identity)

    def one(lap, state):
        source = count - 1 - lap if reverse else lap
        return combine(
            state, jax.tree.map(lambda a: lax.dynamic_index_in_dim(a, source, 0, False), gathered)
        )

    return lax.fori_loop(0, ahead, one, state)


def extended_2(cells, sides, width):
    for axis, dim in sides:
        count = lax.axis_size(axis)
        head = lax.slice_in_dim(cells, 0, width, axis=dim)
        tail = lax.slice_in_dim(cells, cells.shape[dim] - width, cells.shape[dim], axis=dim)
        cells = jnp.concatenate(
            [
                lax.ppermute(tail, axis, [(i, (i + 1) % count) for i in range(count)]),
                cells,
                lax.ppermute(head, axis, [((i + 1) % count, i) for i in range(count)]),
            ],
            axis=dim,
        )
    return cells


def compose(earlier, later):
    return (earlier[0] * later[0], later[0] * earlier[1] + later[1])


def decay_power(steps):
    magnitude = jnp.abs(steps)
    parity = jnp.where(magnitude % 2 == 0, 1.0, -1.0).astype(jnp.float32)
    return parity * jnp.exp(magnitude.astype(jnp.float32) * math.log(abs(root_value)))


def build_stencil(length, reach_cells):
    source_index = lax.broadcasted_iota(jnp.int32, (length + 2 * reach_cells, length), 0)
    target_index = lax.broadcasted_iota(jnp.int32, (length + 2 * reach_cells, length), 1)
    offset = source_index - reach_cells - target_index
    values = first_coeff * (decay_power(offset - 1) - decay_power(offset + 1))
    values = values + second_coeff * (decay_power(offset - 2) - decay_power(offset + 2))
    return jnp.where(jnp.abs(offset) <= reach_cells, inverse_gain * values, 0.0)


def apply_stencil(extended, stencil, length):
    flat = extended.reshape((-1, extended.shape[-1]))
    product = jnp.dot(
        flat, stencil, precision=lax.Precision.HIGHEST, preferred_element_type=jnp.float32
    )
    return product.reshape(extended.shape[:-1] + (length,))


def local(cotangent, lower, pivot, speed):
    fields, planes, height, length = cotangent.shape
    log_keep = jnp.log(lower)
    inclusive = jnp.cumsum(log_keep, axis=1)
    exclusive = inclusive - log_keep
    summed = inclusive[:, -1]
    row_index = lax.broadcasted_iota(jnp.int32, (height, height), 0)
    col_index = lax.broadcasted_iota(jnp.int32, (height, height), 1)
    lower_part = (row_index >= col_index)[None]
    exponent = exclusive[:, :, None] - exclusive[:, None, :]
    factor = jnp.where(lower_part, jnp.exp(jnp.where(lower_part, exponent, 0.0)), 0.0)
    rising_base = jnp.einsum("fji,fzix->fzjx", factor, cotangent, precision=lax.Precision.HIGHEST)
    entry_gain = jnp.exp(exclusive)
    leave_gain = jnp.exp(summed[:, None] - exclusive)
    scaled_base = rising_base / pivot[:, None, :, None]
    settle_base = jnp.einsum("fij,fzix->fzjx", factor, scaled_base, precision=lax.Precision.HIGHEST)
    spread = jnp.einsum("fij,fi->fj", factor, entry_gain / pivot, precision=lax.Precision.HIGHEST)
    through = jnp.exp(summed)
    lift_out = lower[:, -1][:, None, None] * rising_base[:, :, -1, :]
    spread_first = spread[:, 0]
    settle_first = settle_base[:, :, 0, :]
    through_map = through[:, None, None]
    identity_pair = (jnp.ones_like(through_map), jnp.zeros_like(lift_out))
    rise_result = prefix((through_map, lift_out), "wall", compose, identity_pair, False)
    incoming = rise_result[1]
    crest_top = settle_first + incoming * spread_first[:, None, None]
    fall_result = prefix((through_map, crest_top), "wall", compose, identity_pair, True)
    descent = fall_result[1]
    adjoint = settle_base + incoming[:, :, None, :] * spread[:, None, :, None]
    adjoint = adjoint + descent[:, :, None, :] * leave_gain[:, None, :, None]
    reach_cells = 24
    stencil = build_stencil(length, reach_cells)
    speed_grid = speed[:, None, :, None]
    flux_field = speed_grid * adjoint
    extended = extended_2(flux_field, (("stream", 3),), reach_cells)
    state_grad = adjoint + apply_stencil(extended, stencil, length)
    return state_grad


def solution(mesh):
    return jax.shard_map(
        local,
        mesh=mesh,
        in_specs=(
            P(None, None, "wall", "stream"),
            P(None, "wall"),
            P(None, "wall"),
            P(None, "wall"),
        ),
        out_specs=P(None, None, "wall", "stream"),
        check_vma=False,
    )
```

profile of v0, /device:TPU:0, one launch (start us, length us, event | category | flops | bytes accessed | tf_op | source)
XLA Modules:
  0.0 117.6 jit_solution(14755371114347931901)
XLA Ops:
  0.0 0.0 copy-start
  0.0 0.8 log.3
  0.9 0.9 slice_reduce_fusion
  1.7 0.2 reduce_window_sum.11
  1.9 0.2 exponential_reduce_fusion
  2.1 0.7 divide_bitcast_fusion
  2.8 0.3 fusion.85
  3.2 0.1 copy.27
  3.2 0.0 copy-done
  3.3 0.0 copy-start.4
  3.3 2.5 %convolution_bitcast_fusion = f32[5,16,32,256]{3,2,1,0:T(8,128)S(1)} fusion(f32[5,16,32,256]{3,2,1,0:T(8,128)S(1)} %copy-done, f32[5,32]{1,0:T(8,128)S(1)} %get-tuple-element.188, pred[32,32]{0,1:T(8,128)(4,1)S(1)} %iota_compare_fusion), kind=kOutput, calls=%fused_computation.16 | convolution fusion | flops 251673600 | bytes 5244544 | tf_op jit(solution)/shard_map/fji,fzix->fzjx/dot_general | solution.py:84
  5.8 0.0 copy-done.4
  5.8 0.0 copy-start.5
  5.8 2.6 %fusion.12 = f32[5,16,32,256]{3,2,1,0:T(8,128)S(1)} fusion(f32[5,16,32,256]{3,2,1,0:T(8,128)S(1)} %convolution_bitcast_fusion, f32[5,32]{1,0:T(8,128)S(1)} %copy-done.4, f32[5,32]{1,0:T(8,128)S(1)} %get-tuple-element.188, pred[32,32]{0,1:T(8,128)(4,1)S(1)} %iota_compare_fusion), kind=kOutput, calls=%fused_computation.15 | convolution fusion | flops 252328960 | bytes 5245184 | tf_op jit(solution)/shard_map/fij,fzix->fzjx/dot_general | solution.py:88
  8.4 0.0 copy-start.2
  8.4 1.5 %copy-done.2 = f32[5,16,32,256]{3,2,1,0:T(8,128)} copy-done((f32[5,16,32,256]{3,2,1,0:T(8,128)}, f32[5,16,32,256]{3,2,1,0:T(8,128)S(1)}, u32[]{:S(2)}) %copy-start.2) | copy-done | bytes 2621464
  9.9 0.0 copy-start.3
  9.9 0.1 slice.29
  10.0 0.1 fusion.82
  10.1 11.6 %all_gather.15 = f32[8,5,16,256]{3,2,1,0:T(8,128)S(1)} all-gather(f32[1,5,16,256]{3,2,1,0:T(8,128)S(1)} %copy.16), channel_id=1, replica_groups=mesh['wall'=8,'stream'=4] {'wall'}, dimensions={0}, use_global_device_ids=true | all-gather | bytes 737280 | tf_op jit(solution)/shard_map/all_gather | solution.py:18
  21.7 0.0 copy-done.5
  21.7 0.6 dynamic-slice
  22.9 0.2 dynamic-update-slice
  23.1 13.2 %all-reduce = f32[40]{0:T(128)S(1)} all-reduce(f32[40]{0:T(128)S(1)} %dynamic-update-slice), channel_id=2, replica_groups=mesh['wall'=8,'stream'=4] {'wall'}, use_global_device_ids=true, to_apply=%add | all-reduce | flops 40 | bytes 320
  36.3 0.1 reshape.44
  36.4 0.1 bitcast_add_fusion.2
  36.5 10.6 %all-gather.1 = f32[40,16,256]{2,1,0:T(8,128)S(1)} all-gather(f32[5,16,256]{2,1,0:T(8,128)S(1)} %bitcast_add_fusion.2), channel_id=3, replica_groups=mesh['wall'=8,'stream'=4] {'wall'}, dimensions={0}, use_global_device_ids=true | all-gather | bytes 737280 | tf_op jit(solution)/shard_map/all_gather | solution.py:18
  47.1 0.9 while.27
  47.1 0.1 bitcast_add_fusion.6
  47.2 0.1 bitcast_add_fusion.6
  47.4 0.1 bitcast_add_fusion.6
  47.5 0.1 bitcast_add_fusion.6
  47.6 0.1 bitcast_add_fusion.6
  47.8 0.1 bitcast_add_fusion.6
  47.9 0.1 bitcast_add_fusion.6
  48.0 0.1 subtract_exponential_fusion
  48.1 0.0 copy-done.3
  48.1 2.4 %fusion.9 = f32[5,16,32,256]{3,2,1,0:T(8,128)S(1)} fusion(f32[5,16,32,256]{3,2,1,0:T(8,128)} %copy-done.2, f32[5,32]{1,0:T(8,128)S(1)} %copy-done.3, f32[5,32]{1,0:T(8,128)S(1)} %subtract_exponential_fusion, f32[5,16,256]{2,1,0:T(8,128)S(1)} %get-tuple-element.134, f32[5,32]{1,0:T(8,128)S(1)} %bitcast.55, f32[5,16,256]{2,1,0:T(8,128)S(1)} %get-tuple-element.133), kind=kLoop, calls=%fused_computation.14 | loop fusion | flops 3276800 | bytes 5408640 | tf_op jit(solution)/shard_map/mul | solution.py:106
  50.5 0.0 copy-start.1
  50.5 1.5 %copy-done.1 = f32[5,16,32,256]{3,2,1,0:T(8,128)} copy-done((f32[5,16,32,256]{3,2,1,0:T(8,128)}, f32[5,16,32,256]{3,2,1,0:T(8,128)S(1)}, u32[]{:S(2)}) %copy-start.1) | copy-done | bytes 2621464
  52.0 2.0 %fusion.116 = (f32[5,16,32,24]{3,2,1,0:T(8,128)}, f32[5,16,32,24]{3,2,1,0:T(8,128)}) fusion(f32[5,16,32,256]{3,2,1,0:T(8,128)S(1)} %fusion.9), kind=kLoop, calls=%fused_computation.145 | loop fusion | bytes 983040 | tf_op jit(solution)/shard_map/slice | solution.py:34
  54.0 2.7 %copy.20 = f32[5,16,32,24]{2,3,1,0:T(8,128)} copy(f32[5,16,32,24]{3,2,1,0:T(8,128)} %get-tuple-element.189) | data formatting | bytes 491520 | tf_op jit(solution)/shard_map/slice | solution.py:34
  56.7 1.6 %collective-permute-start = (f32[5,16,32,24]{2,3,1,0:T(8,128)}, f32[5,16,32,24]{2,3,1,0:T(8,128)}, u32[]{:S(2)}, u32[]{:S(2)}) collective-permute-start(f32[5,16,32,24]{2,3,1,0:T(8,128)} %copy.20), channel_id=1, source_target_pairs={{0,1},{1,2},{2,3},{3,0},{4,5},{5,6},{6,7},{7,4},{8,9},{9,10},{10,1... | collective-permute-start | bytes 737288 | tf_op jit(solution)/shard_map/ppermute | solution.py:37
  58.2 2.7 %copy.21 = f32[5,16,32,24]{2,3,1,0:T(8,128)} copy(f32[5,16,32,24]{3,2,1,0:T(8,128)} %get-tuple-element.190) | data formatting | bytes 491520 | tf_op jit(solution)/shard_map/slice | solution.py:33
  60.9 2.2 %collective-permute-start.1 = (f32[5,16,32,24]{2,3,1,0:T(8,128)}, f32[5,16,32,24]{2,3,1,0:T(8,128)}, u32[]{:S(2)}, u32[]{:S(2)}) collective-permute-start(f32[5,16,32,24]{2,3,1,0:T(8,128)} %copy.21), channel_id=1, source_target_pairs={{1,0},{2,1},{3,2},{0,3},{5,4},{6,5},{7,6},{4,7},{9,8},{10,9},{11,1... | collective-permute-start | bytes 737288 | tf_op jit(solution)/shard_map/ppermute | solution.py:39
  63.2 20.2 %collective-permute-done = f32[5,16,32,24]{2,3,1,0:T(8,128)} collective-permute-done((f32[5,16,32,24]{2,3,1,0:T(8,128)}, f32[5,16,32,24]{2,3,1,0:T(8,128)}, u32[]{:S(2)}, u32[]{:S(2)}) %collective-permute-start) | collective-permute-done | bytes 245792 | tf_op jit(solution)/shard_map/ppermute | solution.py:37
  83.4 2.7 %copy.22 = f32[5,16,32,24]{3,2,1,0:T(8,128)} copy(f32[5,16,32,24]{2,3,1,0:T(8,128)} %collective-permute-done) | data formatting | bytes 491520 | tf_op jit(solution)/shard_map/ppermute | solution.py:37
  86.1 17.7 %collective-permute-done.1 = f32[5,16,32,24]{2,3,1,0:T(8,128)} collective-permute-done((f32[5,16,32,24]{2,3,1,0:T(8,128)}, f32[5,16,32,24]{2,3,1,0:T(8,128)}, u32[]{:S(2)}, u32[]{:S(2)}) %collective-permute-start.1) | collective-permute-done | bytes 245792 | tf_op jit(solution)/shard_map/ppermute | solution.py:39
  103.8 2.7 %copy.23 = f32[5,16,32,24]{3,2,1,0:T(8,128)} copy(f32[5,16,32,24]{2,3,1,0:T(8,128)} %collective-permute-done.1) | data formatting | bytes 491520 | tf_op jit(solution)/shard_map/ppermute | solution.py:39
  106.6 11.0 %fusion.8 = f32[5,16,32,256]{3,2,1,0:T(8,128)} fusion(f32[5,16,32,256]{3,2,1,0:T(8,128)} %copy-done.2, f32[5,16,32,24]{3,2,1,0:T(8,128)} %copy.23, f32[5,16,32,256]{3,2,1,0:T(8,128)} %copy-done.1, f32[5,16,32,24]{3,2,1,0:T(8,128)} %copy.22, f32[5,32]{1,0:T(8,128)S(1)} %subtract_exponential_fusion, f32[5,16,256]{2,1,0:T(8,128)S(1)} %get-tuple-element.134, ...), kind=kOutput, calls=%fused_computation.13 | convolution fusion | flops 2401968128 | bytes 8522176 | tf_op jit(solution)/shard_map/dot_general | solution.py:67
  (16 shorter events, 0.1 us)
Async XLA Ops:
  0.0 3.3 %copy-start = (f32[5,16,32,256]{3,2,1,0:T(8,128)S(1)}, f32[5,16,32,256]{3,2,1,0:T(8,128)}, u32[]{:S(2)}) copy-start(f32[5,16,32,256]{3,2,1,0:T(8,128)} %param.8) | copy-start | bytes 7864324
  3.3 2.5 %copy-start.4 = (f32[5,32]{1,0:T(8,128)S(1)}, f32[5,32]{1,0:T(8,128)}, u32[]{:S(2)}) copy-start(f32[5,32]{1,0:T(8,128)} %param.10) | copy-start | bytes 1924
  5.8 15.9 %copy-start.5 = (u32[32]{0:T(128)S(1)}, u32[32]{0:T(128)}, u32[]{:S(2)}) copy-start(u32[32]{0:T(128)} %constant.118) | copy-start | bytes 388
  8.4 1.5 %copy-start.2 = (f32[5,16,32,256]{3,2,1,0:T(8,128)}, f32[5,16,32,256]{3,2,1,0:T(8,128)S(1)}, u32[]{:S(2)}) copy-start(f32[5,16,32,256]{3,2,1,0:T(8,128)S(1)} %fusion.12) | copy-start | bytes 7864324
  9.9 38.1 %copy-start.3 = (f32[5,32]{1,0:T(8,128)S(1)}, f32[5,32]{1,0:T(8,128)}, u32[]{:S(2)}) copy-start(f32[5,32]{1,0:T(8,128)} %param.11) | copy-start | bytes 1924
  50.5 1.5 %copy-start.1 = (f32[5,16,32,256]{3,2,1,0:T(8,128)}, f32[5,16,32,256]{3,2,1,0:T(8,128)S(1)}, u32[]{:S(2)}) copy-start(f32[5,16,32,256]{3,2,1,0:T(8,128)S(1)} %fusion.9) | copy-start | bytes 7864324
  56.7 26.7 %collective-permute-start = (f32[5,16,32,24]{2,3,1,0:T(8,128)}, f32[5,16,32,24]{2,3,1,0:T(8,128)}, u32[]{:S(2)}, u32[]{:S(2)}) collective-permute-start(f32[5,16,32,24]{2,3,1,0:T(8,128)} %copy.20), channel_id=1, source_target_pairs={{0,1},{1,2},{2,3},{3,0},{4,5},{5,6},{6,7},{7,4},{8,9},{9,10},{10,1... | collective-permute-start | bytes 737288 | tf_op jit(solution)/shard_map/ppermute | solution.py:37
  60.9 42.9 %collective-permute-start.1 = (f32[5,16,32,24]{2,3,1,0:T(8,128)}, f32[5,16,32,24]{2,3,1,0:T(8,128)}, u32[]{:S(2)}, u32[]{:S(2)}) collective-permute-start(f32[5,16,32,24]{2,3,1,0:T(8,128)} %copy.21), channel_id=1, source_target_pairs={{1,0},{2,1},{3,2},{0,3},{5,4},{6,5},{7,6},{4,7},{9,8},{10,9},{11,1... | collective-permute-start | bytes 737288 | tf_op jit(solution)/shard_map/ppermute | solution.py:39
where the time goes:
time: 118 us
  waiting for transfers between devices  37.9 us (32%)
  blocking collectives  35.4 us (30%)
  local copies, waits for them, and re-layouts  18.8 us (16%)
  matrix products  16.5 us (14%)
  other arithmetic  4.19 us (4%)
  starting transfers between devices  3.82 us (3%)
    all_gather x2, blocking collectives, prefix(): gathered = jax.tree.map(lambda a: lax.all_gather(a, axis), part)  22.2 us
    ppermute x1, waiting for transfers between devices, extended_2(): lax.ppermute(tail, axis, [(i, (i + 1) % count) for i in range(count)])  20.2 us
    ppermute x1, waiting for transfers between devices, extended_2(): lax.ppermute(head, axis, [((i + 1) % count, i) for i in range(count)])  17.7 us
    unnamed x1, blocking collectives  13.2 us
    dot_general x1, matrix products, apply_stencil(): jnp.dot(flat, stencil, precision=lax.Precision.HIGHEST, preferred_element...  11 us
    slice x2, local copies, waits for them, and re-layouts, extended_2(): lax.slice_in_dim(cells, cells.shape[dim] - width, cells.shape[dim], axis=...  4.67 us
    unnamed x15, local copies, waits for them, and re-layouts  3.83 us
    ppermute x1, local copies, waits for them, and re-layouts, extended_2(): lax.ppermute(head, axis, [((i + 1) % count, i) for i in range(count)])  2.72 us
  transfers between devices with their start and end apart: 2, of which 2 were waited for; matrix products, arithmetic and copies ran while one was open for 5% of the time, Pallas kernels for 0%

commit v1 on v0

v1 whole, which is shorter than its diff:
```python
import functools
import math

import jax
import jax.numpy as jnp
import ml_dtypes
import numpy as np
from jax import lax
from jax.experimental import pallas as pl
from jax.experimental.pallas import tpu as pltpu
from jax.sharding import PartitionSpec as P

root_value = (math.sqrt(5.0) - 3.0) / 2.0
inverse_gain = 3.0 / math.sqrt(5.0)
first_coeff = 7.0 / 9.0
second_coeff = 1.0 / 36.0
MESH = pl.DeviceIdType.MESH
VMEM_LIMIT = 40 * 1024 * 1024


def up_to(value, unit):
    return -(-value // unit) * unit


def split_np(values):
    high = values.astype(ml_dtypes.bfloat16)
    low = (values - high.astype(np.float64)).astype(ml_dtypes.bfloat16)
    return high, low


def split(values):
    high = values.astype(jnp.bfloat16)
    low = (values - high.astype(jnp.float32)).astype(jnp.bfloat16)
    return high, low


def stream_constants(length):
    r = root_value
    cell = np.arange(length)
    offset = cell[:, None] - cell[None, :]
    power = lambda d: r ** np.abs(d).astype(np.float64)
    inner = first_coeff * (power(offset - 1) - power(offset + 1))
    inner = inverse_gain * (inner + second_coeff * (power(offset - 2) - power(offset + 2)))
    kappa = inverse_gain * (first_coeff * (1 / r - r) + second_coeff * (r**-2 - r**2))
    delta = inverse_gain * second_coeff * (r - 1 / r)
    weights = np.zeros((8, length))
    weights[0] = r ** (length - 1.0 - cell)
    weights[1, length - 1] = 1.0
    weights[2] = r ** (1.0 * cell)
    weights[3, 0] = 1.0
    profile = np.zeros((8, length))
    profile[0] = -kappa * r ** (cell + 1.0)
    profile[1, 0] = -delta
    profile[2] = kappa * r ** (1.0 * length - cell)
    profile[3, length - 1] = delta
    stencil = np.concatenate(split_np(inner), axis=0)
    edges = np.concatenate(split_np(weights), axis=0)
    high, low = split_np(profile)
    profiles = np.concatenate([high, low, high, low], axis=0)
    return stencil, edges, profiles


def exchange_kernel(
    n, streams, fields, planes, rows, length, share,
    cot_hbm, low_ref, pivot_ref, speed_ref, stencil_hbm, edges_ref,
    base_hbm, from_left, from_right,
    cot, settle, base, stencil, sent, got, answer, carried, to_left, to_right,
    load_sem, stencil_sem, store_sem, send1, recv1, send2, recv2, send3, recv3,
):
    wall = lax.axis_index("wall")
    stream = lax.axis_index("stream")
    right = lax.rem(stream + 1, streams)
    left = lax.rem(stream + streams - 1, streams)

    loads = [
        pltpu.make_async_copy(cot_hbm.at[f], cot.at[f], load_sem.at[f]) for f in range(fields)
    ]
    for load in loads:
        load.start()
    stencil_load = pltpu.make_async_copy(stencil_hbm, stencil, stencil_sem)
    stencil_load.start()

    barrier = pltpu.get_barrier_semaphore()
    for d in range(1, n):
        pl.semaphore_signal(
            barrier, inc=1, device_id={"wall": lax.rem(wall + d, n)}, device_id_type=MESH
        )
    for side in (left, right):
        pl.semaphore_signal(barrier, inc=1, device_id={"stream": side}, device_id_type=MESH)

    lanes = 4 * rows
    total = fields * rows
    row_at = lax.rem(lax.broadcasted_iota(jnp.int32, (total, lanes), 0), rows)
    col_at = lax.rem(lax.broadcasted_iota(jnp.int32, (total, lanes), 1), rows)
    small_row = lax.broadcasted_iota(jnp.int32, (rows, rows), 0)
    small_col = lax.broadcasted_iota(jnp.int32, (rows, rows), 1)

    def column(ref, shift):
        pick = small_row == small_col + shift
        return jnp.concatenate(
            [
                jnp.sum(jnp.where(pick, ref[f : f + 1, :], 0.0), axis=1, keepdims=True)
                for f in range(fields)
            ],
            axis=0,
        )

    before = column(low_ref, 1)
    inverse_pivot = 1.0 / column(pivot_ref, 0)
    speed = column(speed_ref, 0)
    product = jnp.where(row_at > col_at, before, 1.0)
    step = 1
    while step < rows:
        product = product * jnp.where(row_at >= step, pltpu.roll(product, step, 0), 1.0)
        step *= 2
    factor = jnp.where(row_at >= col_at, product, 0.0)
    weighted = factor * inverse_pivot

    lane = lax.broadcasted_iota(jnp.int32, (rows, lanes), 1)
    wide_row = lax.broadcasted_iota(jnp.int32, (rows, lanes), 0)
    coeff_lane = lax.broadcasted_iota(jnp.int32, (1, length), 1)
    half = length // 2
    operators, spreads, leaves, speeds = [], [], [], []
    coeffs = jnp.zeros((1, length), jnp.float32)
    for f in range(fields):
        span = slice(f * rows, (f + 1) * rows)
        gram = lax.dot_general(
            weighted[span], factor[span], (((0,), (0,)), ((), ())),
            precision=lax.Precision.HIGHEST, preferred_element_type=jnp.float32,
        )[:rows]
        last = low_ref[f : f + 1, rows - 1 : rows]
        leave_row = factor[(f + 1) * rows - 1 : (f + 1) * rows] * last
        leave = jnp.sum(jnp.where(lane == wide_row, leave_row, 0.0), axis=1, keepdims=True)
        spread = gram[:, 0:1]
        coeffs = coeffs + jnp.where(coeff_lane == f, leave_row[:, 0:1], 0.0)
        coeffs = coeffs + jnp.where(coeff_lane == half + f, spread[0:1], 0.0)
        extra = jnp.where(wide_row[:16] == 0, leave_row, 0.0)
        stacked = jnp.concatenate([gram, extra], axis=0)
        high = stacked.astype(jnp.bfloat16).astype(jnp.float32)
        low_or_high = jnp.where(
            lax.broadcasted_iota(jnp.int32, (rows + 16, lanes), 1) < 2 * rows, high, stacked - high
        )
        operators.append(low_or_high.astype(jnp.bfloat16))
        spreads.append(jnp.broadcast_to(spread, (rows, length)))
        leaves.append(jnp.broadcast_to(leave, (rows, length)))
        speeds.append(jnp.broadcast_to(speed[span], (rows, length)))
    for o in range(n):
        depth = sent.shape[1] - 2 * share
        sent[o, 2 * share :, :] = jnp.broadcast_to(coeffs, (depth, length))

    for f in range(fields):
        loads[f].wait()
        for z in range(planes):
            line = f * planes + z
            high, low = split(cot[f, z])
            out = jnp.dot(
                operators[f],
                jnp.concatenate([high, low, high, low], axis=0),
                preferred_element_type=jnp.float32,
            )
            settle[f, z] = out[:rows]
            sent[line // share, line % share, :] = out[rows]
            sent[line // share, share + line % share, :] = out[0]

    pl.semaphore_wait(barrier, n + 1)

    def swap(source, target, send, recv, d):
        peer = lax.rem(wall + d, n)
        return pltpu.make_async_remote_copy(
            src_ref=source.at[peer], dst_ref=target.at[wall],
            send_sem=send.at[peer], recv_sem=recv.at[wall],
            device_id={"wall": peer}, device_id_type=MESH,
        )

    def arrive(source, target, send, recv, d):
        peer = lax.rem(wall + d, n)
        pltpu.make_async_remote_copy(
            src_ref=source.at[peer], dst_ref=target.at[peer],
            send_sem=send.at[peer], recv_sem=recv.at[peer],
            device_id={"wall": peer}, device_id_type=MESH,
        ).wait_recv()

    first = [swap(sent, got, send1, recv1, d) for d in range(1, n)]
    for copy in first:
        copy.start()
    got[wall] = sent[wall]
    for d in range(1, n):
        arrive(sent, got, send1, recv1, d)

    line_field = (wall * share + lax.broadcasted_iota(jnp.int32, (share, length), 0)) // planes
    share_lane = lax.broadcasted_iota(jnp.int32, (share, length), 1)
    incoming = jnp.zeros((share, length), jnp.float32)
    through, crest = [], []
    for b in range(n):
        coeff_row = got[b, 2 * share : 2 * share + 1, :]
        t = jnp.sum(jnp.where(share_lane == line_field, coeff_row, 0.0), axis=1, keepdims=True)
        p = jnp.sum(
            jnp.where(share_lane == line_field + half, coeff_row, 0.0), axis=1, keepdims=True
        )
        answer[b, 0:share, :] = incoming
        through.append(t)
        crest.append(got[b, share : 2 * share, :] + p * incoming)
        incoming = t * incoming + got[b, 0:share, :]
    descent = jnp.zeros((share, length), jnp.float32)
    pad = answer.shape[1] - 2 * share
    for b in range(n - 1, -1, -1):
        answer[b, share : 2 * share, :] = descent
        if pad:
            answer[b, 2 * share :, :] = jnp.zeros((pad, length), jnp.float32)
        descent = through[b] * descent + crest[b]

    second = [swap(answer, carried, send2, recv2, d) for d in range(1, n)]
    for copy in second:
        copy.start()
    carried[wall] = answer[wall]
    stencil_load.wait()
    for d in range(1, n):
        arrive(answer, carried, send2, recv2, d)

    edges = edges_ref[...]
    for f in range(fields):
        for z in range(planes):
            line = f * planes + z
            at = line // share, line % share
            up = carried[at[0], at[1] : at[1] + 1, :]
            down = carried[at[0], share + at[1] : share + at[1] + 1, :]
            adjoint = settle[f, z] + spreads[f] * up + leaves[f] * down
            base[f, z] = adjoint
            settle[f, z] = speeds[f] * adjoint
        high, low = split(settle[f].reshape(planes * rows, length))
        dims = (((1,), (1,)), ((), ()))
        sums = lax.dot_general(edges, high, dims, preferred_element_type=jnp.float32)
        rest = lax.dot_general(edges, low, dims, preferred_element_type=jnp.float32)
        sums = sums[:8] + sums[8:] + rest[:8]
        to_right[f] = sums[0:2]
        to_left[f] = sums[2:4]

    third = [
        pltpu.make_async_remote_copy(
            src_ref=source, dst_ref=target, send_sem=send3.at[i], recv_sem=recv3.at[i],
            device_id={"stream": side}, device_id_type=MESH,
        )
        for i, (source, target, side) in enumerate(
            ((to_right, from_left, right), (to_left, from_right, left))
        )
    ]
    for copy in third:
        copy.start()

    stores = []
    for f in range(fields):
        high, low = split(settle[f].reshape(planes * rows, length))
        slope = jnp.dot(high, stencil[:length], preferred_element_type=jnp.float32)
        slope = slope + jnp.dot(low, stencil[:length], preferred_element_type=jnp.float32)
        slope = slope + jnp.dot(high, stencil[length:], preferred_element_type=jnp.float32)
        base[f] = base[f] + slope.reshape(planes, rows, length)
        store = pltpu.make_async_copy(base.at[f], base_hbm.at[f], store_sem.at[f])
        store.start()
        stores.append(store)
    for copy in first + second:
        copy.wait_send()
    for copy in third:
        copy.wait()
    for store in stores:
        store.wait()


def halo_kernel(planes, rows, length, base_ref, left_ref, right_ref, profile_ref, out_ref):
    blank = jnp.zeros((4, planes * rows), jnp.float32)
    sums = jnp.concatenate([left_ref[0], right_ref[0], blank], axis=0)
    high = sums.astype(jnp.bfloat16).astype(jnp.float32)
    stacked = jnp.concatenate([high, high, sums - high, sums - high], axis=0).astype(jnp.bfloat16)
    halo = lax.dot_general(
        stacked, profile_ref[...], (((0,), (0,)), ((), ())), preferred_element_type=jnp.float32
    )
    out_ref[0] = base_ref[0] + halo.reshape(planes, rows, length)


def local(n, streams, cotangent, lower, pivot, speed):
    fields, planes, rows, length = cotangent.shape
    share = -(-fields * planes // n)
    stencil, edges, profiles = stream_constants(length)
    depth1 = up_to(2 * share + 1, 8)
    depth2 = up_to(2 * share, 8)
    edge_shape = (fields, 2, planes * rows)
    vmem = pl.BlockSpec(memory_space=pltpu.VMEM)
    hbm = pl.BlockSpec(memory_space=pl.ANY)
    f32 = jnp.float32
    dma = pltpu.SemaphoreType.DMA
    base, from_left, from_right = pl.pallas_call(
        functools.partial(exchange_kernel, n, streams, fields, planes, rows, length, share),
        out_shape=(
            jax.ShapeDtypeStruct(cotangent.shape, f32),
            jax.ShapeDtypeStruct(edge_shape, f32),
            jax.ShapeDtypeStruct(edge_shape, f32),
        ),
        in_specs=[hbm, vmem, vmem, vmem, hbm, vmem],
        out_specs=(hbm, vmem, vmem),
        scratch_shapes=[
            pltpu.VMEM(cotangent.shape, f32),
            pltpu.VMEM(cotangent.shape, f32),
            pltpu.VMEM(cotangent.shape, f32),
            pltpu.VMEM(stencil.shape, jnp.bfloat16),
            pltpu.VMEM((n, depth1, length), f32),
            pltpu.VMEM((n, depth1, length), f32),
            pltpu.VMEM((n, depth2, length), f32),
            pltpu.VMEM((n, depth2, length), f32),
            pltpu.VMEM(edge_shape, f32),
            pltpu.VMEM(edge_shape, f32),
            dma((fields,)),
            dma,
            dma((fields,)),
            dma((n,)),
            dma((n,)),
            dma((n,)),
            dma((n,)),
            dma((2,)),
            dma((2,)),
        ],
        compiler_params=pltpu.CompilerParams(
            collective_id=0, has_side_effects=True, vmem_limit_bytes=VMEM_LIMIT
        ),
    )(cotangent, lower, pivot, speed, jnp.asarray(stencil), jnp.asarray(edges))
    block = pl.BlockSpec((1, planes, rows, length), lambda f: (f, 0, 0, 0))
    side = pl.BlockSpec((1,) + edge_shape[1:], lambda f: (f, 0, 0))
    profile_spec = pl.BlockSpec(profiles.shape, lambda f: (0, 0))
    return pl.pallas_call(
        functools.partial(halo_kernel, planes, rows, length),
        grid=(fields,),
        out_shape=jax.ShapeDtypeStruct(cotangent.shape, f32),
        in_specs=[block, side, side, profile_spec],
        out_specs=block,
        compiler_params=pltpu.CompilerParams(vmem_limit_bytes=VMEM_LIMIT),
    )(base, from_left, from_right, jnp.asarray(profiles))


def solution(mesh):
    return jax.shard_map(
        functools.partial(local, mesh.shape["wall"], mesh.shape["stream"]),
        mesh=mesh,
        in_specs=(
            P(None, None, "wall", "stream"),
            P(None, "wall"),
            P(None, "wall"),
            P(None, "wall"),
        ),
        out_specs=P(None, None, "wall", "stream"),
        check_vma=False,
    )
```

time: 118 us -> 28.4 us (0.24)
  waiting for transfers between devices: 37.9 us -> 0 us
  blocking collectives: 35.4 us -> 0 us
  Pallas kernels: 0 us -> 22.6 us
  matrix products: 16.5 us -> 0 us
  local copies, waits for them, and re-layouts: 18.8 us -> 5.45 us
  other arithmetic: 4.19 us -> 0 us
  starting transfers between devices: 3.82 us -> 0 us
    ppermute x2 -> x0, waiting for transfers between devices: 37.9 us -> none  [the longest x1 20.2 us: extended_2(): lax.ppermute(tail, axis, [(i, (i + 1) % count) for i in range(count)])]
    pallas_call x0 -> x2, Pallas kernels: none -> 22.6 us  [the longest x1 19.4 us: local(): pl.pallas_call(functools.partial(exchange_kernel, n, streams, fields, pla...]
    all_gather x2 -> x0, blocking collectives: 22.2 us -> none  [prefix(): gathered = jax.tree.map(lambda a: lax.all_gather(a, axis), part)]
    dot_general x4 -> x0, matrix products: 16.5 us -> none  [the longest x1 11 us: apply_stencil(): jnp.dot(flat, stencil, precision=lax.Precision.HIGHEST, preferred_element...]
    unnamed x1 -> x0, blocking collectives: 13.2 us -> none
    slice x5 -> x0, local copies, waits for them, and re-layouts: 8.28 us -> none  [the longest x2 4.67 us: extended_2(): lax.slice_in_dim(cells, cells.shape[dim] - width, cells.shape[dim], axis=...]
    ppermute x2 -> x0, local copies, waits for them, and re-layouts: 5.44 us -> none  [the longest x1 2.72 us: extended_2(): lax.ppermute(head, axis, [((i + 1) % count, i) for i in range(count)])]
    ppermute x2 -> x0, starting transfers between devices: 3.82 us -> none  [the longest x1 2.25 us: extended_2(): lax.ppermute(head, axis, [((i + 1) % count, i) for i in range(count)])]
  transfers between devices with their start and end apart: 2 -> 0, of which waited for: 2 -> 0; matrix products, arithmetic and copies ran while one was open for 5% -> 0% of each run, Pallas kernels for 0% -> 0%
where the time goes in v1:
time: 28.4 us; the launch traced here: 28 us
  Pallas kernels  22.6 us (80%)
  local copies, waits for them, and re-layouts  5.45 us (19%)
    pallas_call x1, Pallas kernels, local(): pl.pallas_call(functools.partial(exchange_kernel, n, streams, fields, pla...  19.4 us
    unnamed x14, local copies, waits for them, and re-layouts  5.45 us
    pallas_call x1, Pallas kernels, local(): pl.pallas_call(functools.partial(halo_kernel, planes, rows, length), grid...  3.19 us

profile of v1, /device:TPU:0, one launch (start us, length us, event | category | flops | bytes accessed | tf_op | source)
XLA Modules:
  0.0 28.0 jit_solution(4023078396111785892)
XLA Ops:
  0.0 0.0 copy-start
  0.0 1.7 %copy-done = f32[5,16,32,256]{3,2,1,0:T(8,128)S(1)} copy-done((f32[5,16,32,256]{3,2,1,0:T(8,128)S(1)}, f32[5,16,32,256]{3,2,1,0:T(8,128)}, u32[]{:S(2)}) %copy-start) | copy-done | bytes 2621464
  1.7 0.0 copy-start.1
  1.7 0.9 %copy-done.1 = bf16[512,256]{1,0:T(8,128)(2,1)S(1)} copy-done((bf16[512,256]{1,0:T(8,128)(2,1)S(1)}, bf16[512,256]{1,0:T(8,128)(2,1)}, u32[]{:S(2)}) %copy-start.1) | copy-done | bytes 262168
  2.7 0.0 copy-start.3
  2.7 0.7 %copy-done.3 = bf16[16,256]{1,0:T(8,128)(2,1)S(1)} copy-done((bf16[16,256]{1,0:T(8,128)(2,1)S(1)}, bf16[16,256]{1,0:T(8,128)(2,1)}, u32[]{:S(2)}) %copy-start.3) | copy-done | bytes 8216
  3.4 0.0 copy-start.4
  3.4 0.7 %copy-done.4 = f32[5,32]{1,0:T(8,128)S(1)} copy-done((f32[5,32]{1,0:T(8,128)S(1)}, f32[5,32]{1,0:T(8,128)}, u32[]{:S(2)}) %copy-start.4) | copy-done | bytes 664
  4.1 0.0 copy-start.5
  4.1 0.7 %copy-done.5 = f32[5,32]{1,0:T(8,128)S(1)} copy-done((f32[5,32]{1,0:T(8,128)S(1)}, f32[5,32]{1,0:T(8,128)}, u32[]{:S(2)}) %copy-start.5) | copy-done | bytes 664
  4.8 0.0 copy-start.6
  4.8 0.7 %copy-done.6 = f32[5,32]{1,0:T(8,128)S(1)} copy-done((f32[5,32]{1,0:T(8,128)S(1)}, f32[5,32]{1,0:T(8,128)}, u32[]{:S(2)}) %copy-start.6) | copy-done | bytes 664
  5.5 0.0 copy-start.2
  5.5 19.4 %shard_map.73 = (f32[5,16,32,256]{3,2,1,0:T(8,128)S(1)}, f32[5,2,512]{2,1,0:T(2,128)S(1)}, f32[5,2,512]{2,1,0:T(2,128)S(1)}) custom-call(f32[5,16,32,256]{3,2,1,0:T(8,128)S(1)} %copy-done, f32[5,32]{1,0:T(8,128)S(1)} %copy-done.4, f32[5,32]{1,0:T(8,128)S(1)} %copy-done.5, f32[5,32]{1,0:T(8,128)S(1)} %copy-done.6, bf16[512,256]{1,0:T(8,128)(2,1)S(1)} %copy-done.1, ...), custom_call_target="tpu_custom_call" | custom-call | tf_op jit(solution)/shard_map/pallas_call | solution.py:290
  24.8 0.0 copy-done.2
  24.9 3.2 %shard_map.74 = f32[5,16,32,256]{3,2,1,0:T(8,128)} custom-call(f32[5,16,32,256]{3,2,1,0:T(8,128)S(1)} %get-tuple-element.8.base_ref, f32[5,2,512]{2,1,0:T(2,128)S(1)} %get-tuple-element.9.left_ref, f32[5,2,512]{2,1,0:T(2,128)S(1)} %get-tuple-element.10.right_ref, bf16[32,256]{1,0:T(8,128)(2,1)S(1)} %copy-done.2), custom_call_target="tpu_custom_call" | custom-call | tf_op jit(solution)/shard_map/pallas_call | solution.py:327
Async XLA Ops:
  0.0 1.7 %copy-start = (f32[5,16,32,256]{3,2,1,0:T(8,128)S(1)}, f32[5,16,32,256]{3,2,1,0:T(8,128)}, u32[]{:S(2)}) copy-start(f32[5,16,32,256]{3,2,1,0:T(8,128)} %cot_hbm.1) | copy-start | bytes 7864324
  1.7 0.9 %copy-start.1 = (bf16[512,256]{1,0:T(8,128)(2,1)S(1)}, bf16[512,256]{1,0:T(8,128)(2,1)}, u32[]{:S(2)}) copy-start(bf16[512,256]{1,0:T(8,128)(2,1)} %constant.6.clone.stencil_hbm) | copy-start | bytes 786436
  2.7 0.7 %copy-start.3 = (bf16[16,256]{1,0:T(8,128)(2,1)S(1)}, bf16[16,256]{1,0:T(8,128)(2,1)}, u32[]{:S(2)}) copy-start(bf16[16,256]{1,0:T(8,128)(2,1)} %constant.7.clone.edges_ref) | copy-start | bytes 24580
  3.4 0.7 %copy-start.4 = (f32[5,32]{1,0:T(8,128)S(1)}, f32[5,32]{1,0:T(8,128)}, u32[]{:S(2)}) copy-start(f32[5,32]{1,0:T(8,128)} %low_ref.1) | copy-start | bytes 1924
  4.1 0.7 %copy-start.5 = (f32[5,32]{1,0:T(8,128)S(1)}, f32[5,32]{1,0:T(8,128)}, u32[]{:S(2)}) copy-start(f32[5,32]{1,0:T(8,128)} %pivot_ref.1) | copy-start | bytes 1924
  4.8 0.7 %copy-start.6 = (f32[5,32]{1,0:T(8,128)S(1)}, f32[5,32]{1,0:T(8,128)}, u32[]{:S(2)}) copy-start(f32[5,32]{1,0:T(8,128)} %speed_ref.1) | copy-start | bytes 1924
  5.5 19.4 %copy-start.2 = (bf16[32,256]{1,0:T(8,128)(2,1)S(1)}, bf16[32,256]{1,0:T(8,128)(2,1)}, u32[]{:S(2)}) copy-start(bf16[32,256]{1,0:T(8,128)(2,1)} %constant.8.clone.profile_ref) | copy-start | bytes 49156

commit v2 on v1

--- a/solution.py
+++ b/solution.py
@@ -3,8 +3,6 @@
 
 import jax
 import jax.numpy as jnp
-import ml_dtypes
-import numpy as np
 from jax import lax
 from jax.experimental import pallas as pl
 from jax.experimental.pallas import tpu as pltpu
@@ -22,63 +20,80 @@
     return -(-value // unit) * unit
 
 
-def split_np(values):
-    high = values.astype(ml_dtypes.bfloat16)
-    low = (values - high.astype(np.float64)).astype(ml_dtypes.bfloat16)
-    return high, low
-
-
 def split(values):
     high = values.astype(jnp.bfloat16)
     low = (values - high.astype(jnp.float32)).astype(jnp.bfloat16)
     return high, low
 
 
-def stream_constants(length):
-    r = root_value
-    cell = np.arange(length)
-    offset = cell[:, None] - cell[None, :]
-    power = lambda d: r ** np.abs(d).astype(np.float64)
-    inner = first_coeff * (power(offset - 1) - power(offset + 1))
-    inner = inverse_gain * (inner + second_coeff * (power(offset - 2) - power(offset + 2)))
-    kappa = inverse_gain * (first_coeff * (1 / r - r) + second_coeff * (r**-2 - r**2))
-    delta = inverse_gain * second_coeff * (r - 1 / r)
-    weights = np.zeros((8, length))
-    weights[0] = r ** (length - 1.0 - cell)
-    weights[1, length - 1] = 1.0
-    weights[2] = r ** (1.0 * cell)
-    weights[3, 0] = 1.0
-    profile = np.zeros((8, length))
-    profile[0] = -kappa * r ** (cell + 1.0)
-    profile[1, 0] = -delta
-    profile[2] = kappa * r ** (1.0 * length - cell)
-    profile[3, length - 1] = delta
-    stencil = np.concatenate(split_np(inner), axis=0)
-    edges = np.concatenate(split_np(weights), axis=0)
-    high, low = split_np(profile)
-    profiles = np.concatenate([high, low, high, low], axis=0)
-    return stencil, edges, profiles
+def root_power(steps):
+    even = steps - 2.0 * jnp.floor(steps * 0.5) == 0.0
+    size = jnp.exp(steps * math.log(-root_value))
+    return jnp.where(even, size, -size)
+
+
+far_scale = inverse_gain * (
+    first_coeff * (1.0 / root_value - root_value)
+    + second_coeff * (root_value**-2 - root_value**2)
+)
+near_shift = inverse_gain * second_coeff * (root_value - 1.0 / root_value)
+
+
+def stencil_block(length):
+    source = lax.broadcasted_iota(jnp.int32, (length, length), 0)
+    target = lax.broadcasted_iota(jnp.int32, (length, length), 1)
+    offset = source - target
+    steps = jnp.abs(offset).astype(jnp.float32)
+    size = far_scale * root_power(steps) + jnp.where(steps == 1.0, near_shift, 0.0)
+    return jnp.where(offset > 0, size, jnp.where(offset < 0, -size, 0.0))
+
+
+def edge_weights(length):
+    row = lax.broadcasted_iota(jnp.int32, (8, length), 0)
+    cell = lax.broadcasted_iota(jnp.int32, (8, length), 1)
+    back = length - 1 - cell
+    decay = root_power(jnp.where(row == 0, back, cell).astype(jnp.float32))
+    edge = jnp.where(jnp.where(row == 1, back, cell) == 0, 1.0, 0.0)
+    weights = jnp.where((row == 0) | (row == 2), decay, edge)
+    return jnp.where(row < 4, weights, 0.0)
+
+
+def edge_profiles(length):
+    row = lax.broadcasted_iota(jnp.int32, (8, length), 0)
+    cell = lax.broadcasted_iota(jnp.int32, (8, length), 1)
+    back = length - 1 - cell
+    depth = jnp.where(row < 2, cell, back)
+    decay = far_scale * root_power((depth + 1).astype(jnp.float32))
+    edge = jnp.where(depth == 0, near_shift, 0.0)
+    profile = jnp.where((row == 0) | (row == 2), decay, edge)
+    return jnp.where(row < 2, -profile, jnp.where(row < 4, profile, 0.0))
 
 
 def exchange_kernel(
     n, streams, fields, planes, rows, length, share,
-    cot_hbm, low_ref, pivot_ref, speed_ref, stencil_hbm, edges_ref,
-    base_hbm, from_left, from_right,
-    cot, settle, base, stencil, sent, got, answer, carried, to_left, to_right,
-    load_sem, stencil_sem, store_sem, send1, recv1, send2, recv2, send3, recv3,
+    cot_hbm, low_hbm, pivot_hbm, speed_hbm,
+    base, from_left, from_right,
+    cot, settle, low_ref, pivot_ref, speed_ref, sent, got, answer, carried, to_left, to_right,
+    load_sem, row_sem, send1, recv1, send2, recv2, send3, recv3,
 ):
     wall = lax.axis_index("wall")
     stream = lax.axis_index("stream")
     right = lax.rem(stream + 1, streams)
     left = lax.rem(stream + streams - 1, streams)
 
+    row_loads = [
+        pltpu.make_async_copy(source, target, row_sem.at[i])
+        for i, (source, target) in enumerate(
+            ((low_hbm, low_ref), (pivot_hbm, pivot_ref), (speed_hbm, speed_ref))
+        )
+    ]
+    for load in row_loads:
+        load.start()
     loads = [
         pltpu.make_async_copy(cot_hbm.at[f], cot.at[f], load_sem.at[f]) for f in range(fields)
     ]
     for load in loads:
         load.start()
-    stencil_load = pltpu.make_async_copy(stencil_hbm, stencil, stencil_sem)
-    stencil_load.start()
 
     barrier = pltpu.get_barrier_semaphore()
     for d in range(1, n):
@@ -105,6 +120,8 @@
             axis=0,
         )
 
+    for load in row_loads:
+        load.wait()
     before = column(low_ref, 1)
     inverse_pivot = 1.0 / column(pivot_ref, 0)
     speed = column(speed_ref, 0)
@@ -213,11 +230,13 @@
     for copy in second:
         copy.start()
     carried[wall] = answer[wall]
-    stencil_load.wait()
+    stencil_high, stencil_low = split(stencil_block(length))
+    weights = edge_weights(length)
+    high = weights.astype(jnp.bfloat16).astype(jnp.float32)
+    edges = jnp.concatenate([high, weights - high], axis=0).astype(jnp.bfloat16)
     for d in range(1, n):
         arrive(answer, carried, send2, recv2, d)
 
-    edges = edges_ref[...]
     for f in range(fields):
         for z in range(planes):
             line = f * planes + z
@@ -247,44 +266,51 @@
     for copy in third:
         copy.start()
 
-    stores = []
     for f in range(fields):
         high, low = split(settle[f].reshape(planes * rows, length))
-        slope = jnp.dot(high, stencil[:length], preferred_element_type=jnp.float32)
-        slope = slope + jnp.dot(low, stencil[:length], preferred_element_type=jnp.float32)
-        slope = slope + jnp.dot(high, stencil[length:], preferred_element_type=jnp.float32)
+        slope = jnp.dot(high, stencil_high, preferred_element_type=jnp.float32)
+        slope = slope + jnp.dot(low, stencil_high, preferred_element_type=jnp.float32)
+        slope = slope + jnp.dot(high, stencil_low, preferred_element_type=jnp.float32)
         base[f] = base[f] + slope.reshape(planes, rows, length)
-        store = pltpu.make_async_copy(base.at[f], base_hbm.at[f], store_sem.at[f])
-        store.start()
-        stores.append(store)
     for copy in first + second:
         copy.wait_send()
     for copy in third:
         copy.wait()
+
+
+def halo_kernel(
+    fields, planes, rows, length, base, from_left, from_right, out_hbm, out, store_sem
+):
+    profile = edge_profiles(length)
+    high = profile.astype(jnp.bfloat16).astype(jnp.float32)
+    profiles = jnp.concatenate([high, profile - high, high, profile - high], axis=0)
+    profiles = profiles.astype(jnp.bfloat16)
+    blank = jnp.zeros((4, planes * rows), jnp.float32)
+    stores = []
+    for f in range(fields):
+        sums = jnp.concatenate([from_left[f], from_right[f], blank], axis=0)
+        high = sums.astype(jnp.bfloat16).astype(jnp.float32)
+        rest = sums - high
+        stacked = jnp.concatenate([high, high, rest, rest], axis=0).astype(jnp.bfloat16)
+        halo = lax.dot_general(
+            stacked, profiles, (((0,), (0,)), ((), ())), preferred_element_type=jnp.float32
+        )
+        out[f] = base[f] + halo.reshape(planes, rows, length)
+        store = pltpu.make_async_copy(out.at[f], out_hbm.at[f], store_sem.at[f])
+        store.start()
+        stores.append(store)
     for store in stores:
         store.wait()
-
-
-def halo_kernel(planes, rows, length, base_ref, left_ref, right_ref, profile_ref, out_ref):
-    blank = jnp.zeros((4, planes * rows), jnp.float32)
-    sums = jnp.concatenate([left_ref[0], right_ref[0], blank], axis=0)
-    high = sums.astype(jnp.bfloat16).astype(jnp.float32)
-    stacked = jnp.concatenate([high, high, sums - high, sums - high], axis=0).astype(jnp.bfloat16)
-    halo = lax.dot_general(
-        stacked, profile_ref[...], (((0,), (0,)), ((), ())), preferred_element_type=jnp.float32
-    )
-    out_ref[0] = base_ref[0] + halo.reshape(planes, rows, length)
 
 
 def local(n, streams, cotangent, lower, pivot, speed):
     fields, planes, rows, length = cotangent.shape
     share = -(-fields * planes // n)
-    stencil, edges, profiles = stream_constants(length)
     depth1 = up_to(2 * share + 1, 8)
     depth2 = up_to(2 * share, 8)
     edge_shape = (fields, 2, planes * rows)
     vmem = pl.BlockSpec(memory_space=pltpu.VMEM)
-    hbm = pl.BlockSpec(memory_space=pl.ANY)
+    hbm = pl.BlockSpec(memory_space=pltpu.HBM)
     f32 = jnp.float32
     dma = pltpu.SemaphoreType.DMA
     base, from_left, from_right = pl.pallas_call(
@@ -294,13 +320,14 @@
             jax.ShapeDtypeStruct(edge_shape, f32),
             jax.ShapeDtypeStruct(edge_shape, f32),
         ),
-        in_specs=[hbm, vmem, vmem, vmem, hbm, vmem],
-        out_specs=(hbm, vmem, vmem),
+        in_specs=[hbm] * 4,
+        out_specs=(vmem, vmem, vmem),
         scratch_shapes=[
             pltpu.VMEM(cotangent.shape, f32),
             pltpu.VMEM(cotangent.shape, f32),
-            pltpu.VMEM(cotangent.shape, f32),
-            pltpu.VMEM(stencil.shape, jnp.bfloat16),
+            pltpu.VMEM(lower.shape, f32),
+            pltpu.VMEM(lower.shape, f32),
+            pltpu.VMEM(lower.shape, f32),
             pltpu.VMEM((n, depth1, length), f32),
             pltpu.VMEM((n, depth1, length), f32),
             pltpu.VMEM((n, depth2, length), f32),
@@ -308,8 +335,7 @@
             pltpu.VMEM(edge_shape, f32),
             pltpu.VMEM(edge_shape, f32),
             dma((fields,)),
-            dma,
-            dma((fields,)),
+            dma((3,)),
             dma((n,)),
             dma((n,)),
             dma((n,)),
@@ -320,18 +346,15 @@
         compiler_params=pltpu.CompilerParams(
             collective_id=0, has_side_effects=True, vmem_limit_bytes=VMEM_LIMIT
         ),
-    )(cotangent, lower, pivot, speed, jnp.asarray(stencil), jnp.asarray(edges))
-    block = pl.BlockSpec((1, planes, rows, length), lambda f: (f, 0, 0, 0))
-    side = pl.BlockSpec((1,) + edge_shape[1:], lambda f: (f, 0, 0))
-    profile_spec = pl.BlockSpec(profiles.shape, lambda f: (0, 0))
+    )(*[pltpu.with_memory_space_constraint(a, pltpu.HBM) for a in (cotangent, lower, pivot, speed)])
     return pl.pallas_call(
-        functools.partial(halo_kernel, planes, rows, length),
-        grid=(fields,),
+        functools.partial(halo_kernel, fields, planes, rows, length),
         out_shape=jax.ShapeDtypeStruct(cotangent.shape, f32),
-        in_specs=[block, side, side, profile_spec],
-        out_specs=block,
+        in_specs=[vmem] * 3,
+        out_specs=hbm,
+        scratch_shapes=[pltpu.VMEM(cotangent.shape, f32), dma((fields,))],
         compiler_params=pltpu.CompilerParams(vmem_limit_bytes=VMEM_LIMIT),
-    )(base, from_left, from_right, jnp.asarray(profiles))
+    )(base, from_left, from_right)
 
 
 def solution(mesh):

time: 28.4 us -> 22.5 us (0.79)
  local copies, waits for them, and re-layouts: 5.45 us -> 0 us
  Pallas kernels: 22.6 us -> 22.3 us
    unnamed x14 -> x0, local copies, waits for them, and re-layouts: 5.45 us -> none
    pallas_call x1, Pallas kernels: 3.19 us -> 1.81 us  [local(): pl.pallas_call(functools.partial(halo_kernel, fields, planes, rows, lengt...]
    pallas_call x1, Pallas kernels: 19.4 us -> 20.5 us  [local(): pl.pallas_call(functools.partial(exchange_kernel, n, streams, fields, pla...]
where the time goes in v2:
time: 22.5 us; the launch traced here: 22.3 us
  Pallas kernels  22.3 us (99%)
    pallas_call x1, Pallas kernels, local(): pl.pallas_call(functools.partial(exchange_kernel, n, streams, fields, pla...  20.5 us
    pallas_call x1, Pallas kernels, local(): pl.pallas_call(functools.partial(halo_kernel, fields, planes, rows, lengt...  1.81 us

profile of v2, /device:TPU:0, one launch (start us, length us, event | category | flops | bytes accessed | tf_op | source)
XLA Modules:
  0.0 22.3 jit_solution(5814648084160441554)
XLA Ops:
  0.0 20.5 %shard_map.46 = (f32[5,16,32,256]{3,2,1,0:T(8,128)S(1)}, f32[5,2,512]{2,1,0:T(2,128)S(1)}, f32[5,2,512]{2,1,0:T(2,128)S(1)}) custom-call(f32[5,16,32,256]{3,2,1,0:T(8,128)} %cot_hbm.1, f32[5,32]{1,0:T(8,128)} %low_hbm.1, f32[5,32]{1,0:T(8,128)} %pivot_hbm.1, f32[5,32]{1,0:T(8,128)} %speed_hbm.1), custom_call_target="tpu_custom_call" | custom-call | tf_op jit(solution)/shard_map/pallas_call | solution.py:316
  20.5 1.8 %shard_map.47 = f32[5,16,32,256]{3,2,1,0:T(8,128)} custom-call(f32[5,16,32,256]{3,2,1,0:T(8,128)S(1)} %get-tuple-element.8.base, f32[5,2,512]{2,1,0:T(2,128)S(1)} %get-tuple-element.9.from_left, f32[5,2,512]{2,1,0:T(2,128)S(1)} %get-tuple-element.10.from_right), custom_call_target="tpu_custom_call" | custom-call | tf_op jit(solution)/shard_map/pallas_call | solution.py:350

commit v3 on v2

v3 whole, which is shorter than its diff:
```python
import functools
import math

import jax
import jax.numpy as jnp
from jax import lax
from jax.experimental import pallas as pl
from jax.experimental.pallas import tpu as pltpu
from jax.sharding import PartitionSpec as P

root_value = (math.sqrt(5.0) - 3.0) / 2.0
inverse_gain = 3.0 / math.sqrt(5.0)
first_coeff = 7.0 / 9.0
second_coeff = 1.0 / 36.0
MESH = pl.DeviceIdType.MESH
VMEM_LIMIT = 40 * 1024 * 1024


def up_to(value, unit):
    return -(-value // unit) * unit


def split(values):
    high = values.astype(jnp.bfloat16)
    low = (values - high.astype(jnp.float32)).astype(jnp.bfloat16)
    return high, low


def root_power(steps):
    even = steps - 2.0 * jnp.floor(steps * 0.5) == 0.0
    size = jnp.exp(steps * math.log(-root_value))
    return jnp.where(even, size, -size)


far_scale = inverse_gain * (
    first_coeff * (1.0 / root_value - root_value)
    + second_coeff * (root_value**-2 - root_value**2)
)
near_shift = inverse_gain * second_coeff * (root_value - 1.0 / root_value)


def stencil_block(length):
    source = lax.broadcasted_iota(jnp.int32, (length, length), 0)
    target = lax.broadcasted_iota(jnp.int32, (length, length), 1)
    offset = source - target
    steps = jnp.abs(offset).astype(jnp.float32)
    size = far_scale * root_power(steps) + jnp.where(steps == 1.0, near_shift, 0.0)
    return jnp.where(offset > 0, size, jnp.where(offset < 0, -size, 0.0))


def edge_weights(length):
    row = lax.broadcasted_iota(jnp.int32, (8, length), 0)
    cell = lax.broadcasted_iota(jnp.int32, (8, length), 1)
    back = length - 1 - cell
    decay = root_power(jnp.where(row == 0, back, cell).astype(jnp.float32))
    edge = jnp.where(jnp.where(row == 1, back, cell) == 0, 1.0, 0.0)
    weights = jnp.where((row == 0) | (row == 2), decay, edge)
    return jnp.where(row < 4, weights, 0.0)


def edge_profiles(length):
    row = lax.broadcasted_iota(jnp.int32, (8, length), 0)
    cell = lax.broadcasted_iota(jnp.int32, (8, length), 1)
    back = length - 1 - cell
    depth = jnp.where(row < 2, cell, back)
    decay = far_scale * root_power((depth + 1).astype(jnp.float32))
    edge = jnp.where(depth == 0, near_shift, 0.0)
    profile = jnp.where((row == 0) | (row == 2), decay, edge)
    return jnp.where(row < 2, -profile, jnp.where(row < 4, profile, 0.0))


def stacked_high(values):
    high = values.astype(jnp.bfloat16).astype(jnp.float32)
    rest = values - high
    return jnp.concatenate([high, high, rest, rest], axis=0).astype(jnp.bfloat16)


def stacked_both(values):
    high = values.astype(jnp.bfloat16).astype(jnp.float32)
    rest = values - high
    return jnp.concatenate([high, rest, high, rest], axis=0).astype(jnp.bfloat16)


def down(left, right):
    return lax.dot_general(
        left, right, (((0,), (0,)), ((), ())), preferred_element_type=jnp.float32
    )


def edge_sums(edges, values):
    high, low = split(values)
    dims = (((1,), (1,)), ((), ()))
    sums = lax.dot_general(edges, high, dims, preferred_element_type=jnp.float32)
    rest = lax.dot_general(edges, low, dims, preferred_element_type=jnp.float32)
    return sums[:8] + sums[8:] + rest[:8]


def through_stencil(values, stencil):
    high, low = split(values)
    slope = jnp.dot(high, stencil[0], preferred_element_type=jnp.float32)
    slope = slope + jnp.dot(low, stencil[0], preferred_element_type=jnp.float32)
    return slope + jnp.dot(high, stencil[1], preferred_element_type=jnp.float32)


def exchange_kernel(
    n, streams, fields, planes, rows, length, share, depth, wide,
    cot_hbm, low_hbm, pivot_hbm, speed_hbm,
    base, carried_out, slope_out, columns,
    cot, low_ref, pivot_ref, speed_ref, sent, got, answer, carried,
    lines_left, lines_right, lines_from_left, lines_from_right, ends, ends_got,
    to_left, to_right, from_left, from_right,
    load_sem, row_sem, send1, recv1, send2, recv2, send3, recv3, send4, recv4, send5, recv5,
):
    wall = lax.axis_index("wall")
    stream = lax.axis_index("stream")
    right = lax.rem(stream + 1, streams)
    left = lax.rem(stream + streams - 1, streams)

    row_loads = [
        pltpu.make_async_copy(source, target, row_sem.at[i])
        for i, (source, target) in enumerate(
            ((low_hbm, low_ref), (pivot_hbm, pivot_ref), (speed_hbm, speed_ref))
        )
    ]
    for load in row_loads:
        load.start()
    loads = [
        pltpu.make_async_copy(cot_hbm.at[f], cot.at[f], load_sem.at[f]) for f in range(fields)
    ]
    for load in loads:
        load.start()

    barrier = pltpu.get_barrier_semaphore()
    for d in range(1, n):
        pl.semaphore_signal(
            barrier, inc=1, device_id={"wall": lax.rem(wall + d, n)}, device_id_type=MESH
        )
    for side in (left, right):
        pl.semaphore_signal(barrier, inc=1, device_id={"stream": side}, device_id_type=MESH)

    def swap(source, target, send, recv, d):
        peer = lax.rem(wall + d, n)
        return pltpu.make_async_remote_copy(
            src_ref=source.at[peer], dst_ref=target.at[wall],
            send_sem=send.at[peer], recv_sem=recv.at[wall],
            device_id={"wall": peer}, device_id_type=MESH,
        )

    def arrive(source, target, send, recv, d):
        peer = lax.rem(wall + d, n)
        pltpu.make_async_remote_copy(
            src_ref=source.at[peer], dst_ref=target.at[peer],
            send_sem=send.at[peer], recv_sem=recv.at[peer],
            device_id={"wall": peer}, device_id_type=MESH,
        ).wait_recv()

    def beside(pairs, send, recv):
        return [
            pltpu.make_async_remote_copy(
                src_ref=source, dst_ref=target, send_sem=send.at[i], recv_sem=recv.at[i],
                device_id={"stream": side}, device_id_type=MESH,
            )
            for i, (source, target, side) in enumerate(pairs)
        ]

    sent[...] = jnp.zeros(sent.shape, jnp.float32)
    weights = edge_weights(length)
    high = weights.astype(jnp.bfloat16).astype(jnp.float32)
    edges = jnp.concatenate([high, weights - high], axis=0).astype(jnp.bfloat16)

    lanes = 4 * rows
    total = fields * rows
    row_at = lax.rem(lax.broadcasted_iota(jnp.int32, (total, lanes), 0), rows)
    col_at = lax.rem(lax.broadcasted_iota(jnp.int32, (total, lanes), 1), rows)
    small_row = lax.broadcasted_iota(jnp.int32, (rows, rows), 0)
    small_col = lax.broadcasted_iota(jnp.int32, (rows, rows), 1)

    def column(ref, shift):
        pick = small_row == small_col + shift
        return jnp.concatenate(
            [
                jnp.sum(jnp.where(pick, ref[f : f + 1, :], 0.0), axis=1, keepdims=True)
                for f in range(fields)
            ],
            axis=0,
        )

    for load in row_loads:
        load.wait()
    before = column(low_ref, 1)
    inverse_pivot = 1.0 / column(pivot_ref, 0)
    speed = column(speed_ref, 0)
    product = jnp.where(row_at > col_at, before, 1.0)
    step = 1
    while step < rows:
        product = product * jnp.where(row_at >= step, pltpu.roll(product, step, 0), 1.0)
        step *= 2
    factor = jnp.where(row_at >= col_at, product, 0.0)
    weighted = factor * inverse_pivot

    lane = lax.broadcasted_iota(jnp.int32, (rows, lanes), 1)
    wide_row = lax.broadcasted_iota(jnp.int32, (rows, lanes), 0)
    coeff_lane = lax.broadcasted_iota(jnp.int32, (1, length), 1)
    line_lane = lax.broadcasted_iota(jnp.int32, (1, wide), 1)
    line_index = (line_lane // depth) * share + line_lane % depth
    line_used = (line_lane % depth < share) & (line_index < fields * planes)
    line_field = jnp.where(line_used, line_index // planes, -1)
    half = length // 2
    spreads, leaves, speeds = [], [], []
    coeffs = jnp.zeros((1, length), jnp.float32)
    line_through = jnp.zeros((1, wide), jnp.float32)
    line_first = jnp.zeros((1, wide), jnp.float32)
    for f in range(fields):
        span = slice(f * rows, (f + 1) * rows)
        last = low_ref[f : f + 1, rows - 1 : rows]
        leave_row = factor[(f + 1) * rows - 1 : (f + 1) * rows] * last
        spread_row = jnp.sum(weighted[span] * factor[span, 0:1], axis=0, keepdims=True)
        leave = jnp.sum(jnp.where(lane == wide_row, leave_row, 0.0), axis=1, keepdims=True)
        spread = jnp.sum(jnp.where(lane == wide_row, spread_row, 0.0), axis=1, keepdims=True)
        coeffs = coeffs + jnp.where(coeff_lane == f, leave_row[:, 0:1], 0.0)
        coeffs = coeffs + jnp.where(coeff_lane == half + f, spread_row[:, 0:1], 0.0)
        line_through = line_through + jnp.where(line_field == f, leave_row[:, 0:1], 0.0)
        line_first = line_first + jnp.where(line_field == f, spread_row[:, 0:1], 0.0)
        spreads.append(jnp.broadcast_to(spread, (rows, length)))
        leaves.append(jnp.broadcast_to(leave, (rows, length)))
        speeds.append(jnp.broadcast_to(speed[span], (rows, length)))
        columns[0, f] = spreads[f][:, :128]
        columns[1, f] = leaves[f][:, :128]
        columns[2, f] = spreads[f][:, :128] * speeds[f][:, :128]
        columns[3, f] = leaves[f][:, :128] * speeds[f][:, :128]
    for o in range(n):
        sent[o, 2 * share : 2 * share + 1, :] = coeffs

    for f in range(fields):
        loads[f].wait()
        for z in range(planes):
            line = f * planes + z
            values = cot[f, z]
            sent[line // share, line % share, :] = jnp.sum(values * leaves[f], axis=0)
            sent[line // share, share + line % share, :] = jnp.sum(values * spreads[f], axis=0)

    pl.semaphore_wait(barrier, n + 1)

    first = [swap(sent, got, send1, recv1, d) for d in range(1, n)]
    for copy in first:
        copy.start()
    got[wall] = sent[wall]

    flat = sent[...].reshape(n * depth, length)
    if wide > n * depth:
        flat = jnp.concatenate(
            [flat, jnp.zeros((wide - n * depth, length), jnp.float32)], axis=0
        )
    sums = edge_sums(edges, flat)
    lines_right[...] = sums[0:2]
    lines_left[...] = sums[2:4]
    lines_copies = beside(
        ((lines_right, lines_from_left, right), (lines_left, lines_from_right, left)), send3, recv3
    )
    for copy in lines_copies:
        copy.start()

    def settle_field(f):
        span = slice(f * rows, (f + 1) * rows)
        gram = lax.dot_general(
            weighted[span], factor[span], (((0,), (0,)), ((), ())),
            precision=lax.Precision.HIGHEST, preferred_element_type=jnp.float32,
        )[:rows]
        high = gram.astype(jnp.bfloat16).astype(jnp.float32)
        operator = jnp.where(lane < 2 * rows, high, gram - high).astype(jnp.bfloat16)
        for z in range(planes):
            high, low = split(cot[f, z])
            out = jnp.dot(
                operator,
                jnp.concatenate([high, low, high, low], axis=0),
                preferred_element_type=jnp.float32,
            )
            base[f, z] = out
            cot[f, z] = speeds[f] * out
        sums = edge_sums(edges, cot[f].reshape(planes * rows, length))
        to_right[f] = sums[0:2]
        to_left[f] = sums[2:4]

    early = (fields + 1) // 2
    for f in range(early):
        settle_field(f)

    for copy in lines_copies:
        copy.wait_recv()
    ends[0:2, :] = lines_from_left[...]
    ends[2:4, :] = lines_from_right[...]
    ends[4:5, :] = line_through
    ends[5:6, :] = line_first
    ends[6:8, :] = jnp.zeros((2, wide), jnp.float32)
    gather = [
        pltpu.make_async_remote_copy(
            src_ref=ends, dst_ref=ends_got.at[wall],
            send_sem=send4.at[lax.rem(wall + d, n)], recv_sem=recv4.at[wall],
            device_id={"wall": lax.rem(wall + d, n)}, device_id_type=MESH,
        )
        for d in range(1, n)
    ]
    for copy in gather:
        copy.start()
    ends_got[wall] = ends[...]

    for f in range(early, fields):
        settle_field(f)
    edge_copies = beside(
        ((to_right, from_left, right), (to_left, from_right, left)), send5, recv5
    )
    for copy in edge_copies:
        copy.start()

    for d in range(1, n):
        arrive(sent, got, send1, recv1, d)

    share_field = (wall * share + lax.broadcasted_iota(jnp.int32, (share, length), 0)) // planes
    share_lane = lax.broadcasted_iota(jnp.int32, (share, length), 1)
    incoming = jnp.zeros((share, length), jnp.float32)
    through, crest = [], []
    for b in range(n):
        coeff_row = got[b, 2 * share : 2 * share + 1, :]
        t = jnp.sum(jnp.where(share_lane == share_field, coeff_row, 0.0), axis=1, keepdims=True)
        p = jnp.sum(
            jnp.where(share_lane == share_field + half, coeff_row, 0.0), axis=1, keepdims=True
        )
        answer[b, 0:share, :] = incoming
        through.append(t)
        crest.append(got[b, share : 2 * share, :] + p * incoming)
        incoming = t * incoming + got[b, 0:share, :]
    descent = jnp.zeros((share, length), jnp.float32)
    for b in range(n - 1, -1, -1):
        answer[b, share : 2 * share, :] = descent
        answer[b, 2 * share :, :] = jnp.zeros((depth - 2 * share, length), jnp.float32)
        descent = through[b] * descent + crest[b]

    second = [swap(answer, carried, send2, recv2, d) for d in range(1, n)]
    for copy in second:
        copy.start()
    carried[wall] = answer[wall]

    stencil = split(stencil_block(length))
    profiles = stacked_both(edge_profiles(length))
    blank = jnp.zeros((4, planes * rows), jnp.float32)
    for copy in edge_copies:
        copy.wait_recv()
    for f in range(fields):
        slope = through_stencil(cot[f].reshape(planes * rows, length), stencil)
        sides = jnp.concatenate([from_left[f], from_right[f], blank], axis=0)
        slope = slope + down(stacked_high(sides), profiles)
        base[f] = base[f] + slope.reshape(planes, rows, length)

    for d in range(1, n):
        peer = lax.rem(wall + d, n)
        pltpu.make_async_remote_copy(
            src_ref=ends, dst_ref=ends_got.at[peer],
            send_sem=send4.at[peer], recv_sem=recv4.at[peer],
            device_id={"wall": peer}, device_id_type=MESH,
        ).wait_recv()
    zero = jnp.zeros((8, wide), jnp.float32)
    incoming, taken_up, through, crest = zero, zero, [], []
    for b in range(n):
        arrived = ends_got[b]
        t, p = arrived[4:5], arrived[5:6]
        taken_up = jnp.where(wall == b, incoming, taken_up)
        through.append(t)
        crest.append(pltpu.roll(arrived, wide - share, 1) + p * incoming)
        incoming = t * incoming + arrived
    descent, taken_down = zero, zero
    for b in range(n - 1, -1, -1):
        taken_down = jnp.where(wall == b, descent, taken_down)
        descent = through[b] * descent + crest[b]
    side_rows = lax.broadcasted_iota(jnp.int32, (8, wide), 0) < 4
    used = side_rows & line_used
    taken_up = jnp.where(used, taken_up, 0.0)
    taken_down = jnp.where(used, taken_down, 0.0)
    halo = down(stacked_high(taken_up + pltpu.roll(taken_down, share, 1)), profiles)

    for d in range(1, n):
        arrive(answer, carried, send2, recv2, d)
    flat = carried[...].reshape(n * depth, length)
    slope = through_stencil(flat, stencil) + halo[: n * depth]
    carried_out[...] = carried[...]
    slope_out[...] = slope.reshape(n, depth, length)

    for copy in first + second + lines_copies + gather + edge_copies:
        copy.wait_send()


def gather_kernel(
    fields, planes, rows, length, share, base, carried, slopes, columns, out_hbm, out, store_sem
):
    stores = []
    for f in range(fields):
        spread, leave, spread_speed, leave_speed = (
            jnp.concatenate([columns[i, f]] * (length // 128), axis=1) for i in range(4)
        )
        for z in range(planes):
            line = f * planes + z
            o, up = line // share, line % share
            low = share + up
            value = base[f, z] + spread * carried[o, up : up + 1, :]
            value = value + leave * carried[o, low : low + 1, :]
            value = value + spread_speed * slopes[o, up : up + 1, :]
            out[f, z] = value + leave_speed * slopes[o, low : low + 1, :]
        store = pltpu.make_async_copy(out.at[f], out_hbm.at[f], store_sem.at[f])
        store.start()
        stores.append(store)
    for store in stores:
        store.wait()


def local(n, streams, cotangent, lower, pivot, speed):
    fields, planes, rows, length = cotangent.shape
    share = -(-fields * planes // n)
    depth = up_to(2 * share + 1, 8)
    wide = up_to(n * depth, 128)
    edge_shape = (fields, 2, planes * rows)
    line_shape = (n, depth, length)
    column_shape = (4, fields, rows, 128)
    vmem = pl.BlockSpec(memory_space=pltpu.VMEM)
    hbm = pl.BlockSpec(memory_space=pltpu.HBM)
    f32 = jnp.float32
    dma = pltpu.SemaphoreType.DMA
    scratch = lambda shape: pltpu.VMEM(shape, f32)
    out_shapes = (cotangent.shape, line_shape, line_shape, column_shape)
    parts = pl.pallas_call(
        functools.partial(
            exchange_kernel, n, streams, fields, planes, rows, length, share, depth, wide
        ),
        out_shape=tuple(jax.ShapeDtypeStruct(shape, f32) for shape in out_shapes),
        in_specs=[hbm] * 4,
        out_specs=(vmem,) * 4,
        scratch_shapes=[scratch(cotangent.shape)]
        + [scratch(lower.shape)] * 3
        + [scratch(line_shape)] * 4
        + [scratch((2, wide))] * 4
        + [scratch((8, wide)), scratch((n, 8, wide))]
        + [scratch(edge_shape)] * 4
        + [dma((fields,)), dma((3,))]
        + [dma((n,))] * 4
        + [dma((2,))] * 2
        + [dma((n,))] * 2
        + [dma((2,))] * 2,
        compiler_params=pltpu.CompilerParams(
            collective_id=0, has_side_effects=True, vmem_limit_bytes=VMEM_LIMIT
        ),
    )(*[
        pltpu.with_memory_space_constraint(a, pltpu.HBM)
        for a in (cotangent, lower, pivot, speed)
    ])
    return pl.pallas_call(
        functools.partial(gather_kernel, fields, planes, rows, length, share),
        out_shape=jax.ShapeDtypeStruct(cotangent.shape, f32),
        in_specs=[vmem] * 4,
        out_specs=hbm,
        scratch_shapes=[scratch(cotangent.shape), dma((fields,))],
        compiler_params=pltpu.CompilerParams(vmem_limit_bytes=VMEM_LIMIT),
    )(*parts)


def solution(mesh):
    return jax.shard_map(
        functools.partial(local, mesh.shape["wall"], mesh.shape["stream"]),
        mesh=mesh,
        in_specs=(
            P(None, None, "wall", "stream"),
            P(None, "wall"),
            P(None, "wall"),
            P(None, "wall"),
        ),
        out_specs=P(None, None, "wall", "stream"),
        check_vma=False,
    )
```

time: 22.5 us -> 18.6 us (0.83)
  Pallas kernels: 22.3 us -> 18.5 us
    pallas_call x1, Pallas kernels: 20.5 us -> 16.8 us  [local(): pl.pallas_call(functools.partial(exchange_kernel, n, streams, fields, pla...]
where the time goes in v3:
time: 18.6 us; the launch traced here: 18.5 us
  Pallas kernels  18.5 us (99%)
    pallas_call x1, Pallas kernels, local(): pl.pallas_call(functools.partial(exchange_kernel, n, streams, fields, pla...  16.8 us
    pallas_call x1, Pallas kernels, local(): pl.pallas_call(functools.partial(gather_kernel, fields, planes, rows, len...  1.67 us

profile of v3, /device:TPU:0, one launch (start us, length us, event | category | flops | bytes accessed | tf_op | source)
XLA Modules:
  0.0 18.5 jit_solution(15431270019876583472)
XLA Ops:
  0.0 16.8 %shard_map.46 = (f32[5,16,32,256]{3,2,1,0:T(8,128)S(1)}, f32[8,24,256]{2,1,0:T(8,128)S(1)}, f32[8,24,256]{2,1,0:T(8,128)S(1)}, f32[4,5,32,128]{3,2,1,0:T(8,128)S(1)}) custom-call(f32[5,16,32,256]{3,2,1,0:T(8,128)} %cot_hbm.1, f32[5,32]{1,0:T(8,128)} %low_hbm.1, f32[5,32]{1,0:T(8,128)} %pivot_hbm.1, f32[5,32]{1,0:T(8,128)} %speed_hbm.1), custom_call_target="tpu_custom_call" | custom-call | tf_op jit(solution)/shard_map/pallas_call | solution.py:428
  16.8 1.7 %shard_map.47 = f32[5,16,32,256]{3,2,1,0:T(8,128)} custom-call(f32[5,16,32,256]{3,2,1,0:T(8,128)S(1)} %get-tuple-element.9.base, f32[8,24,256]{2,1,0:T(8,128)S(1)} %get-tuple-element.10.carried, f32[8,24,256]{2,1,0:T(8,128)S(1)} %get-tuple-element.11.slopes, f32[4,5,32,128]{3,2,1,0:T(8,128)S(1)} %get-tuple-element.12.columns), custom_call_target="tpu_custom_call" | custom-call | tf_op jit(solution)/shard_map/pallas_call | solution.py:453

commit v4 on v3

--- a/solution.py
+++ b/solution.py
@@ -108,7 +108,7 @@
     base, carried_out, slope_out, columns,
     cot, low_ref, pivot_ref, speed_ref, sent, got, answer, carried,
     lines_left, lines_right, lines_from_left, lines_from_right, ends, ends_got,
-    to_left, to_right, from_left, from_right,
+    to_left, to_right, from_left, from_right, stencil,
     load_sem, row_sem, send1, recv1, send2, recv2, send3, recv3, send4, recv4, send5, recv5,
 ):
     wall = lax.axis_index("wall")
@@ -167,6 +167,10 @@
     weights = edge_weights(length)
     high = weights.astype(jnp.bfloat16).astype(jnp.float32)
     edges = jnp.concatenate([high, weights - high], axis=0).astype(jnp.bfloat16)
+
+    for i, part in enumerate(split(stencil_block(length))):
+        stencil[i] = part
+    profiles = stacked_both(edge_profiles(length))
 
     lanes = 4 * rows
     total = fields * rows
@@ -281,9 +285,41 @@
         to_right[f] = sums[0:2]
         to_left[f] = sums[2:4]
 
-    early = (fields + 1) // 2
-    for f in range(early):
+    for f in range(fields):
         settle_field(f)
+    edge_copies = beside(
+        ((to_right, from_left, right), (to_left, from_right, left)), send5, recv5
+    )
+    for copy in edge_copies:
+        copy.start()
+
+    for d in range(1, n):
+        arrive(sent, got, send1, recv1, d)
+
+    share_field = (wall * share + lax.broadcasted_iota(jnp.int32, (share, length), 0)) // planes
+    share_lane = lax.broadcasted_iota(jnp.int32, (share, length), 1)
+    incoming = jnp.zeros((share, length), jnp.float32)
+    through, crest = [], []
+    for b in range(n):
+        coeff_row = got[b, 2 * share : 2 * share + 1, :]
+        t = jnp.sum(jnp.where(share_lane == share_field, coeff_row, 0.0), axis=1, keepdims=True)
+        p = jnp.sum(
+            jnp.where(share_lane == share_field + half, coeff_row, 0.0), axis=1, keepdims=True
+        )
+        answer[b, 0:share, :] = incoming
+        through.append(t)
+        crest.append(got[b, share : 2 * share, :] + p * incoming)
+        incoming = t * incoming + got[b, 0:share, :]
+    descent = jnp.zeros((share, length), jnp.float32)
+    for b in range(n - 1, -1, -1):
+        answer[b, share : 2 * share, :] = descent
+        answer[b, 2 * share :, :] = jnp.zeros((depth - 2 * share, length), jnp.float32)
+        descent = through[b] * descent + crest[b]
+
+    second = [swap(answer, carried, send2, recv2, d) for d in range(1, n)]
+    for copy in second:
+        copy.start()
+    carried[wall] = answer[wall]
 
     for copy in lines_copies:
         copy.wait_recv()
@@ -304,51 +340,20 @@
         copy.start()
     ends_got[wall] = ends[...]
 
-    for f in range(early, fields):
-        settle_field(f)
-    edge_copies = beside(
-        ((to_right, from_left, right), (to_left, from_right, left)), send5, recv5
-    )
-    for copy in edge_copies:
-        copy.start()
-
-    for d in range(1, n):
-        arrive(sent, got, send1, recv1, d)
-
-    share_field = (wall * share + lax.broadcasted_iota(jnp.int32, (share, length), 0)) // planes
-    share_lane = lax.broadcasted_iota(jnp.int32, (share, length), 1)
-    incoming = jnp.zeros((share, length), jnp.float32)
-    through, crest = [], []
-    for b in range(n):
-        coeff_row = got[b, 2 * share : 2 * share + 1, :]
-        t = jnp.sum(jnp.where(share_lane == share_field, coeff_row, 0.0), axis=1, keepdims=True)
-        p = jnp.sum(
-            jnp.where(share_lane == share_field + half, coeff_row, 0.0), axis=1, keepdims=True
-        )
-        answer[b, 0:share, :] = incoming
-        through.append(t)
-        crest.append(got[b, share : 2 * share, :] + p * incoming)
-        incoming = t * incoming + got[b, 0:share, :]
-    descent = jnp.zeros((share, length), jnp.float32)
-    for b in range(n - 1, -1, -1):
-        answer[b, share : 2 * share, :] = descent
-        answer[b, 2 * share :, :] = jnp.zeros((depth - 2 * share, length), jnp.float32)
-        descent = through[b] * descent + crest[b]
-
-    second = [swap(answer, carried, send2, recv2, d) for d in range(1, n)]
-    for copy in second:
-        copy.start()
-    carried[wall] = answer[wall]
-
-    stencil = split(stencil_block(length))
-    profiles = stacked_both(edge_profiles(length))
     blank = jnp.zeros((4, planes * rows), jnp.float32)
-    for copy in edge_copies:
-        copy.wait_recv()
+    ready = fields // 2
     for f in range(fields):
+        if f == ready:
+            for copy in edge_copies:
+                copy.wait_recv()
         slope = through_stencil(cot[f].reshape(planes * rows, length), stencil)
+        if f >= ready:
+            sides = jnp.concatenate([from_left[f], from_right[f], blank], axis=0)
+            slope = slope + down(stacked_high(sides), profiles)
+        base[f] = base[f] + slope.reshape(planes, rows, length)
+    for f in range(ready):
         sides = jnp.concatenate([from_left[f], from_right[f], blank], axis=0)
-        slope = slope + down(stacked_high(sides), profiles)
+        slope = down(stacked_high(sides), profiles)
         base[f] = base[f] + slope.reshape(planes, rows, length)
 
     for d in range(1, n):
@@ -392,6 +397,7 @@
     fields, planes, rows, length, share, base, carried, slopes, columns, out_hbm, out, store_sem
 ):
     stores = []
+    piece = math.gcd(planes, 4)
     for f in range(fields):
         spread, leave, spread_speed, leave_speed = (
             jnp.concatenate([columns[i, f]] * (length // 128), axis=1) for i in range(4)
@@ -404,9 +410,13 @@
             value = value + leave * carried[o, low : low + 1, :]
             value = value + spread_speed * slopes[o, up : up + 1, :]
             out[f, z] = value + leave_speed * slopes[o, low : low + 1, :]
-        store = pltpu.make_async_copy(out.at[f], out_hbm.at[f], store_sem.at[f])
-        store.start()
-        stores.append(store)
+            if z % piece == piece - 1:
+                part = pl.ds(z + 1 - piece, piece)
+                store = pltpu.make_async_copy(
+                    out.at[f, part], out_hbm.at[f, part], store_sem.at[len(stores)]
+                )
+                store.start()
+                stores.append(store)
     for store in stores:
         store.wait()
 
@@ -438,6 +448,7 @@
         + [scratch((2, wide))] * 4
         + [scratch((8, wide)), scratch((n, 8, wide))]
         + [scratch(edge_shape)] * 4
+        + [pltpu.VMEM((2, length, length), jnp.bfloat16)]
         + [dma((fields,)), dma((3,))]
         + [dma((n,))] * 4
         + [dma((2,))] * 2
@@ -455,7 +466,7 @@
         out_shape=jax.ShapeDtypeStruct(cotangent.shape, f32),
         in_specs=[vmem] * 4,
         out_specs=hbm,
-        scratch_shapes=[scratch(cotangent.shape), dma((fields,))],
+        scratch_shapes=[scratch(cotangent.shape), dma((fields * planes,))],
         compiler_params=pltpu.CompilerParams(vmem_limit_bytes=VMEM_LIMIT),
     )(*parts)
 

time: 18.6 us -> 18.2 us (0.978)
  Pallas kernels: 18.5 us -> 18.1 us
    pallas_call x1, Pallas kernels: 16.8 us -> 15.9 us  [local(): pl.pallas_call(functools.partial(exchange_kernel, n, streams, fields, pla...]
    pallas_call x1, Pallas kernels: 1.67 us -> 2.22 us  [local(): pl.pallas_call(functools.partial(gather_kernel, fields, planes, rows, len...]
where the time goes in v4:
time: 18.2 us; the launch traced here: 18.1 us
  Pallas kernels  18.1 us (99%)
    pallas_call x1, Pallas kernels, local(): pl.pallas_call(functools.partial(exchange_kernel, n, streams, fields, pla...  15.9 us
    pallas_call x1, Pallas kernels, local(): pl.pallas_call(functools.partial(gather_kernel, fields, planes, rows, len...  2.22 us

profile of v4, /device:TPU:0, one launch (start us, length us, event | category | flops | bytes accessed | tf_op | source)
XLA Modules:
  0.0 18.1 jit_solution(17056815323347470329)
XLA Ops:
  0.0 15.9 %shard_map.46 = (f32[5,16,32,256]{3,2,1,0:T(8,128)S(1)}, f32[8,24,256]{2,1,0:T(8,128)S(1)}, f32[8,24,256]{2,1,0:T(8,128)S(1)}, f32[4,5,32,128]{3,2,1,0:T(8,128)S(1)}) custom-call(f32[5,16,32,256]{3,2,1,0:T(8,128)} %cot_hbm.1, f32[5,32]{1,0:T(8,128)} %low_hbm.1, f32[5,32]{1,0:T(8,128)} %pivot_hbm.1, f32[5,32]{1,0:T(8,128)} %speed_hbm.1), custom_call_target="tpu_custom_call" | custom-call | tf_op jit(solution)/shard_map/pallas_call | solution.py:438
  15.9 2.2 %shard_map.47 = f32[5,16,32,256]{3,2,1,0:T(8,128)} custom-call(f32[5,16,32,256]{3,2,1,0:T(8,128)S(1)} %get-tuple-element.9.base, f32[8,24,256]{2,1,0:T(8,128)S(1)} %get-tuple-element.10.carried, f32[8,24,256]{2,1,0:T(8,128)S(1)} %get-tuple-element.11.slopes, f32[4,5,32,128]{3,2,1,0:T(8,128)S(1)} %get-tuple-element.12.columns), custom_call_target="tpu_custom_call" | custom-call | tf_op jit(solution)/shard_map/pallas_call | solution.py:464

commit v5 on v4

--- a/solution.py
+++ b/solution.py
@@ -49,13 +49,13 @@
 
 
 def edge_weights(length):
-    row = lax.broadcasted_iota(jnp.int32, (8, length), 0)
-    cell = lax.broadcasted_iota(jnp.int32, (8, length), 1)
-    back = length - 1 - cell
-    decay = root_power(jnp.where(row == 0, back, cell).astype(jnp.float32))
-    edge = jnp.where(jnp.where(row == 1, back, cell) == 0, 1.0, 0.0)
-    weights = jnp.where((row == 0) | (row == 2), decay, edge)
-    return jnp.where(row < 4, weights, 0.0)
+    cell = lax.broadcasted_iota(jnp.int32, (length, 128), 0)
+    odd = lax.broadcasted_iota(jnp.int32, (length, 128), 1) % 2 == 1
+    sides = []
+    for depth in (length - 1 - cell, cell):
+        edge = jnp.where(depth == 0, 1.0, 0.0)
+        sides.append(jnp.where(odd, edge, root_power(depth.astype(jnp.float32))))
+    return jnp.concatenate(sides, axis=1)
 
 
 def edge_profiles(length):
@@ -69,30 +69,9 @@
     return jnp.where(row < 2, -profile, jnp.where(row < 4, profile, 0.0))
 
 
-def stacked_high(values):
-    high = values.astype(jnp.bfloat16).astype(jnp.float32)
-    rest = values - high
-    return jnp.concatenate([high, high, rest, rest], axis=0).astype(jnp.bfloat16)
-
-
 def stacked_both(values):
-    high = values.astype(jnp.bfloat16).astype(jnp.float32)
-    rest = values - high
-    return jnp.concatenate([high, rest, high, rest], axis=0).astype(jnp.bfloat16)
-
-
-def down(left, right):
-    return lax.dot_general(
-        left, right, (((0,), (0,)), ((), ())), preferred_element_type=jnp.float32
-    )
-
-
-def edge_sums(edges, values):
     high, low = split(values)
-    dims = (((1,), (1,)), ((), ()))
-    sums = lax.dot_general(edges, high, dims, preferred_element_type=jnp.float32)
-    rest = lax.dot_general(edges, low, dims, preferred_element_type=jnp.float32)
-    return sums[:8] + sums[8:] + rest[:8]
+    return jnp.concatenate([high, low, high, low], axis=0)
 
 
 def through_stencil(values, stencil):
@@ -103,13 +82,12 @@
 
 
 def exchange_kernel(
-    n, streams, fields, planes, rows, length, share, depth, wide,
+    n, streams, fields, planes, rows, length, share, depth, pack,
     cot_hbm, low_hbm, pivot_hbm, speed_hbm,
     base, carried_out, slope_out, columns,
     cot, low_ref, pivot_ref, speed_ref, sent, got, answer, carried,
-    lines_left, lines_right, lines_from_left, lines_from_right, ends, ends_got,
-    to_left, to_right, from_left, from_right, stencil,
-    load_sem, row_sem, send1, recv1, send2, recv2, send3, recv3, send4, recv4, send5, recv5,
+    ends, ends_got, line_sums, to_left, to_right, from_left, from_right, stencil, weights, profiles,
+    load_sem, row_sem, send1, recv1, send2, recv2, send3, recv3, send4, recv4,
 ):
     wall = lax.axis_index("wall")
     stream = lax.axis_index("stream")
@@ -164,13 +142,10 @@
         ]
 
     sent[...] = jnp.zeros(sent.shape, jnp.float32)
-    weights = edge_weights(length)
-    high = weights.astype(jnp.bfloat16).astype(jnp.float32)
-    edges = jnp.concatenate([high, weights - high], axis=0).astype(jnp.bfloat16)
-
+    for i, part in enumerate(split(edge_weights(length))):
+        weights[i] = part
     for i, part in enumerate(split(stencil_block(length))):
         stencil[i] = part
-    profiles = stacked_both(edge_profiles(length))
 
     lanes = 4 * rows
     total = fields * rows
@@ -205,15 +180,14 @@
     lane = lax.broadcasted_iota(jnp.int32, (rows, lanes), 1)
     wide_row = lax.broadcasted_iota(jnp.int32, (rows, lanes), 0)
     coeff_lane = lax.broadcasted_iota(jnp.int32, (1, length), 1)
-    line_lane = lax.broadcasted_iota(jnp.int32, (1, wide), 1)
-    line_index = (line_lane // depth) * share + line_lane % depth
-    line_used = (line_lane % depth < share) & (line_index < fields * planes)
-    line_field = jnp.where(line_used, line_index // planes, -1)
+    groups = -(-fields // pack)
+    place = lax.broadcasted_iota(jnp.int32, (1, 256), 1) % 128
+    place_field = place // (2 * planes)
     half = length // 2
     spreads, leaves, speeds = [], [], []
     coeffs = jnp.zeros((1, length), jnp.float32)
-    line_through = jnp.zeros((1, wide), jnp.float32)
-    line_first = jnp.zeros((1, wide), jnp.float32)
+    line_through = [jnp.zeros((1, 256), jnp.float32)] * groups
+    line_first = [jnp.zeros((1, 256), jnp.float32)] * groups
     for f in range(fields):
         span = slice(f * rows, (f + 1) * rows)
         last = low_ref[f : f + 1, rows - 1 : rows]
@@ -223,8 +197,9 @@
         spread = jnp.sum(jnp.where(lane == wide_row, spread_row, 0.0), axis=1, keepdims=True)
         coeffs = coeffs + jnp.where(coeff_lane == f, leave_row[:, 0:1], 0.0)
         coeffs = coeffs + jnp.where(coeff_lane == half + f, spread_row[:, 0:1], 0.0)
-        line_through = line_through + jnp.where(line_field == f, leave_row[:, 0:1], 0.0)
-        line_first = line_first + jnp.where(line_field == f, spread_row[:, 0:1], 0.0)
+        here = place_field == f % pack
+        line_through[f // pack] = jnp.where(here, leave_row[:, 0:1], line_through[f // pack])
+        line_first[f // pack] = jnp.where(here, spread_row[:, 0:1], line_first[f // pack])
         spreads.append(jnp.broadcast_to(spread, (rows, length)))
         leaves.append(jnp.broadcast_to(leave, (rows, length)))
         speeds.append(jnp.broadcast_to(speed[span], (rows, length)))
@@ -250,19 +225,40 @@
         copy.start()
     got[wall] = sent[wall]
 
-    flat = sent[...].reshape(n * depth, length)
-    if wide > n * depth:
-        flat = jnp.concatenate(
-            [flat, jnp.zeros((wide - n * depth, length), jnp.float32)], axis=0
-        )
-    sums = edge_sums(edges, flat)
-    lines_right[...] = sums[0:2]
-    lines_left[...] = sums[2:4]
-    lines_copies = beside(
-        ((lines_right, lines_from_left, right), (lines_left, lines_from_right, left)), send3, recv3
+    wide_place = lax.broadcasted_iota(jnp.int32, (rows, 256), 1) % 128 // 2
+    for g in range(groups):
+        tile = jnp.zeros((rows, 256), jnp.float32)
+        for f in range(g * pack, min(fields, (g + 1) * pack)):
+            sums = through_stencil(cot[f].reshape(planes * rows, length), weights)
+            for z in range(planes):
+                mine = wide_place == planes * (f % pack) + z
+                tile = jnp.where(mine, sums[z * rows : (z + 1) * rows], tile)
+        to_right[g] = tile[:, :128]
+        to_left[g] = tile[:, 128:]
+    edge_copies = beside(
+        ((to_right, from_left, right), (to_left, from_right, left)), send3, recv3
     )
-    for copy in lines_copies:
+    for copy in edge_copies:
         copy.start()
+
+    profile = edge_profiles(length)
+    lane_at = lax.broadcasted_iota(jnp.int32, (128, length), 0)
+    profile = jnp.concatenate(
+        [
+            jnp.where(lane_at % 2 == 0, profile[i : i + 1], profile[i + 1 : i + 2])
+            for i in (0, 2)
+        ],
+        axis=0,
+    )
+    high = profile.astype(jnp.bfloat16).astype(jnp.float32)
+    rest = profile - high
+    slot = lax.broadcasted_iota(jnp.int32, (256, length), 0) % 128 // (2 * planes)
+    mixed = jnp.where(slot < 2, high, jnp.where(slot == 2, rest, 0.0))
+    profiles[0] = high.astype(jnp.bfloat16)
+    profiles[1] = rest.astype(jnp.bfloat16)
+    profiles[2] = mixed.astype(jnp.bfloat16)
+
+    operators = []
 
     def settle_field(f):
         span = slice(f * rows, (f + 1) * rows)
@@ -272,6 +268,7 @@
         )[:rows]
         high = gram.astype(jnp.bfloat16).astype(jnp.float32)
         operator = jnp.where(lane < 2 * rows, high, gram - high).astype(jnp.bfloat16)
+        operators.append(operator)
         for z in range(planes):
             high, low = split(cot[f, z])
             out = jnp.dot(
@@ -281,18 +278,9 @@
             )
             base[f, z] = out
             cot[f, z] = speeds[f] * out
-        sums = edge_sums(edges, cot[f].reshape(planes * rows, length))
-        to_right[f] = sums[0:2]
-        to_left[f] = sums[2:4]
 
     for f in range(fields):
         settle_field(f)
-    edge_copies = beside(
-        ((to_right, from_left, right), (to_left, from_right, left)), send5, recv5
-    )
-    for copy in edge_copies:
-        copy.start()
-
     for d in range(1, n):
         arrive(sent, got, send1, recv1, d)
 
@@ -321,13 +309,23 @@
         copy.start()
     carried[wall] = answer[wall]
 
-    for copy in lines_copies:
+    for copy in edge_copies:
         copy.wait_recv()
-    ends[0:2, :] = lines_from_left[...]
-    ends[2:4, :] = lines_from_right[...]
-    ends[4:5, :] = line_through
-    ends[5:6, :] = line_first
-    ends[6:8, :] = jnp.zeros((2, wide), jnp.float32)
+    beyond = [jnp.concatenate([from_left[g], from_right[g]], axis=1) for g in range(groups)]
+    for g in range(groups):
+        lift = jnp.zeros((1, 256), jnp.float32)
+        drop = lift
+        for f in range(g * pack, min(fields, (g + 1) * pack)):
+            here = place_field == f % pack
+            leave, spread = leaves[f][:, :1], spreads[f][:, :1]
+            lift = jnp.where(here, jnp.sum(leave * beyond[g], axis=0, keepdims=True), lift)
+            drop = jnp.where(here, jnp.sum(spread * beyond[g], axis=0, keepdims=True), drop)
+        ends[g : g + 1, :] = lift
+        ends[groups + g : groups + g + 1, :] = drop
+        ends[2 * groups + g : 2 * groups + g + 1, :] = line_through[g]
+        ends[3 * groups + g : 3 * groups + g + 1, :] = line_first[g]
+    if ends.shape[0] > 4 * groups:
+        ends[4 * groups :, :] = jnp.zeros((ends.shape[0] - 4 * groups, 256), jnp.float32)
     gather = [
         pltpu.make_async_remote_copy(
             src_ref=ends, dst_ref=ends_got.at[wall],
@@ -340,20 +338,31 @@
         copy.start()
     ends_got[wall] = ends[...]
 
-    blank = jnp.zeros((4, planes * rows), jnp.float32)
-    ready = fields // 2
+    width = 2 * planes
+    narrow = lax.broadcasted_iota(jnp.int32, (rows, 128), 1)
+    wide_plane = lax.broadcasted_iota(jnp.int32, (rows, 256), 1) % width // 2
     for f in range(fields):
-        if f == ready:
-            for copy in edge_copies:
-                copy.wait_recv()
         slope = through_stencil(cot[f].reshape(planes * rows, length), stencil)
-        if f >= ready:
-            sides = jnp.concatenate([from_left[f], from_right[f], blank], axis=0)
-            slope = slope + down(stacked_high(sides), profiles)
-        base[f] = base[f] + slope.reshape(planes, rows, length)
-    for f in range(ready):
-        sides = jnp.concatenate([from_left[f], from_right[f], blank], axis=0)
-        slope = down(stacked_high(sides), profiles)
+        sums = jnp.dot(
+            operators[f], stacked_both(beyond[f // pack]), preferred_element_type=jnp.float32
+        )
+        sides = []
+        for i in range(2):
+            part = speeds[f][:, :128] * sums[:, 128 * i : 128 * (i + 1)]
+            if f % pack:
+                part = pltpu.roll(part, 128 - width * (f % pack), 1)
+            part = jnp.where(narrow < width, part, 0.0)
+            high = part.astype(jnp.bfloat16).astype(jnp.float32)
+            sides.append(
+                high + pltpu.roll(part - high, width, 1) + pltpu.roll(high, 2 * width, 1)
+            )
+        side = jnp.concatenate(sides, axis=1)
+        spaced = jnp.concatenate(
+            [jnp.where(wide_plane == z, side, 0.0) for z in range(planes)], axis=0
+        )
+        slope = slope + jnp.dot(
+            spaced.astype(jnp.bfloat16), profiles[2], preferred_element_type=jnp.float32
+        )
         base[f] = base[f] + slope.reshape(planes, rows, length)
 
     for d in range(1, n):
@@ -363,33 +372,35 @@
             send_sem=send4.at[peer], recv_sem=recv4.at[peer],
             device_id={"wall": peer}, device_id_type=MESH,
         ).wait_recv()
-    zero = jnp.zeros((8, wide), jnp.float32)
+    zero = jnp.zeros((groups, 256), jnp.float32)
     incoming, taken_up, through, crest = zero, zero, [], []
     for b in range(n):
-        arrived = ends_got[b]
-        t, p = arrived[4:5], arrived[5:6]
+        lift, drop, t, p = (ends_got[b, i * groups : (i + 1) * groups, :] for i in range(4))
         taken_up = jnp.where(wall == b, incoming, taken_up)
         through.append(t)
-        crest.append(pltpu.roll(arrived, wide - share, 1) + p * incoming)
-        incoming = t * incoming + arrived
+        crest.append(drop + p * incoming)
+        incoming = t * incoming + lift
     descent, taken_down = zero, zero
     for b in range(n - 1, -1, -1):
         taken_down = jnp.where(wall == b, descent, taken_down)
         descent = through[b] * descent + crest[b]
-    side_rows = lax.broadcasted_iota(jnp.int32, (8, wide), 0) < 4
-    used = side_rows & line_used
-    taken_up = jnp.where(used, taken_up, 0.0)
-    taken_down = jnp.where(used, taken_down, 0.0)
-    halo = down(stacked_high(taken_up + pltpu.roll(taken_down, share, 1)), profiles)
+    line_sums[...] = jnp.zeros(line_sums.shape, jnp.float32)
+    for line in range(fields * planes):
+        f, z = line // planes, line % planes
+        g, o, up = f // pack, line // share, line % share
+        mine = place // 2 == planes * (f % pack) + z
+        line_sums[o, up : up + 1, :] = jnp.where(mine, taken_up[g : g + 1], 0.0)
+        line_sums[o, share + up : share + up + 1, :] = jnp.where(mine, taken_down[g : g + 1], 0.0)
+    halo = through_stencil(line_sums[...].reshape(n * depth, 256), profiles)
 
     for d in range(1, n):
         arrive(answer, carried, send2, recv2, d)
     flat = carried[...].reshape(n * depth, length)
-    slope = through_stencil(flat, stencil) + halo[: n * depth]
+    slope = through_stencil(flat, stencil) + halo
     carried_out[...] = carried[...]
     slope_out[...] = slope.reshape(n, depth, length)
 
-    for copy in first + second + lines_copies + gather + edge_copies:
+    for copy in first + second + gather + edge_copies:
         copy.wait_send()
 
 
@@ -397,7 +408,6 @@
     fields, planes, rows, length, share, base, carried, slopes, columns, out_hbm, out, store_sem
 ):
     stores = []
-    piece = math.gcd(planes, 4)
     for f in range(fields):
         spread, leave, spread_speed, leave_speed = (
             jnp.concatenate([columns[i, f]] * (length // 128), axis=1) for i in range(4)
@@ -410,13 +420,9 @@
             value = value + leave * carried[o, low : low + 1, :]
             value = value + spread_speed * slopes[o, up : up + 1, :]
             out[f, z] = value + leave_speed * slopes[o, low : low + 1, :]
-            if z % piece == piece - 1:
-                part = pl.ds(z + 1 - piece, piece)
-                store = pltpu.make_async_copy(
-                    out.at[f, part], out_hbm.at[f, part], store_sem.at[len(stores)]
-                )
-                store.start()
-                stores.append(store)
+        store = pltpu.make_async_copy(out.at[f], out_hbm.at[f], store_sem.at[f])
+        store.start()
+        stores.append(store)
     for store in stores:
         store.wait()
 
@@ -425,8 +431,10 @@
     fields, planes, rows, length = cotangent.shape
     share = -(-fields * planes // n)
     depth = up_to(2 * share + 1, 8)
-    wide = up_to(n * depth, 128)
-    edge_shape = (fields, 2, planes * rows)
+    pack = 128 // (2 * planes)
+    groups = -(-fields // pack)
+    end_rows = up_to(4 * groups, 8)
+    edge_shape = (groups, rows, 128)
     line_shape = (n, depth, length)
     column_shape = (4, fields, rows, 128)
     vmem = pl.BlockSpec(memory_space=pltpu.VMEM)
@@ -437,7 +445,7 @@
     out_shapes = (cotangent.shape, line_shape, line_shape, column_shape)
     parts = pl.pallas_call(
         functools.partial(
-            exchange_kernel, n, streams, fields, planes, rows, length, share, depth, wide
+            exchange_kernel, n, streams, fields, planes, rows, length, share, depth, pack
         ),
         out_shape=tuple(jax.ShapeDtypeStruct(shape, f32) for shape in out_shapes),
         in_specs=[hbm] * 4,
@@ -445,15 +453,15 @@
         scratch_shapes=[scratch(cotangent.shape)]
         + [scratch(lower.shape)] * 3
         + [scratch(line_shape)] * 4
-        + [scratch((2, wide))] * 4
-        + [scratch((8, wide)), scratch((n, 8, wide))]
+        + [scratch((end_rows, 256)), scratch((n, end_rows, 256)), scratch((n, depth, 256))]
         + [scratch(edge_shape)] * 4
         + [pltpu.VMEM((2, length, length), jnp.bfloat16)]
+        + [pltpu.VMEM((2, length, 256), jnp.bfloat16)]
+        + [pltpu.VMEM((3, 256, length), jnp.bfloat16)]
         + [dma((fields,)), dma((3,))]
         + [dma((n,))] * 4
         + [dma((2,))] * 2
-        + [dma((n,))] * 2
-        + [dma((2,))] * 2,
+        + [dma((n,))] * 2,
         compiler_params=pltpu.CompilerParams(
             collective_id=0, has_side_effects=True, vmem_limit_bytes=VMEM_LIMIT
         ),
@@ -466,7 +474,7 @@
         out_shape=jax.ShapeDtypeStruct(cotangent.shape, f32),
         in_specs=[vmem] * 4,
         out_specs=hbm,
-        scratch_shapes=[scratch(cotangent.shape), dma((fields * planes,))],
+        scratch_shapes=[scratch(cotangent.shape), dma((fields,))],
         compiler_params=pltpu.CompilerParams(vmem_limit_bytes=VMEM_LIMIT),
     )(*parts)
 

time: 18.2 us -> 18.2 us (level)
    pallas_call x1, Pallas kernels: 15.9 us -> 16.4 us  [local(): pl.pallas_call(functools.partial(exchange_kernel, n, streams, fields, pla...]
    pallas_call x1, Pallas kernels: 2.22 us -> 1.67 us  [local(): pl.pallas_call(functools.partial(gather_kernel, fields, planes, rows, len...]
where the time goes in v5:
time: 18.2 us; the launch traced here: 18.1 us
  Pallas kernels  18.1 us (99%)
    pallas_call x1, Pallas kernels, local(): pl.pallas_call(functools.partial(exchange_kernel, n, streams, fields, pla...  16.4 us
    pallas_call x1, Pallas kernels, local(): pl.pallas_call(functools.partial(gather_kernel, fields, planes, rows, len...  1.67 us

profile of v5, /device:TPU:0, one launch (start us, length us, event | category | flops | bytes accessed | tf_op | source)
XLA Modules:
  0.0 18.1 jit_solution(12549049254234099329)
XLA Ops:
  0.0 16.4 %shard_map.46 = (f32[5,16,32,256]{3,2,1,0:T(8,128)S(1)}, f32[8,24,256]{2,1,0:T(8,128)S(1)}, f32[8,24,256]{2,1,0:T(8,128)S(1)}, f32[4,5,32,128]{3,2,1,0:T(8,128)S(1)}) custom-call(f32[5,16,32,256]{3,2,1,0:T(8,128)} %cot_hbm.1, f32[5,32]{1,0:T(8,128)} %low_hbm.1, f32[5,32]{1,0:T(8,128)} %pivot_hbm.1, f32[5,32]{1,0:T(8,128)} %speed_hbm.1), custom_call_target="tpu_custom_call" | custom-call | tf_op jit(solution)/shard_map/pallas_call | solution.py:446
  16.4 1.7 %shard_map.47 = f32[5,16,32,256]{3,2,1,0:T(8,128)} custom-call(f32[5,16,32,256]{3,2,1,0:T(8,128)S(1)} %get-tuple-element.9.base, f32[8,24,256]{2,1,0:T(8,128)S(1)} %get-tuple-element.10.carried, f32[8,24,256]{2,1,0:T(8,128)S(1)} %get-tuple-element.11.slopes, f32[4,5,32,128]{3,2,1,0:T(8,128)S(1)} %get-tuple-element.12.columns), custom_call_target="tpu_custom_call" | custom-call | tf_op jit(solution)/shard_map/pallas_call | solution.py:472

commit v6 on v5

--- a/solution.py
+++ b/solution.py
@@ -85,7 +85,7 @@
     n, streams, fields, planes, rows, length, share, depth, pack,
     cot_hbm, low_hbm, pivot_hbm, speed_hbm,
     base, carried_out, slope_out, columns,
-    cot, low_ref, pivot_ref, speed_ref, sent, got, answer, carried,
+    cot, settle, row_values, low_ref, pivot_ref, speed_ref, sent, got, answer, carried,
     ends, ends_got, line_sums, to_left, to_right, from_left, from_right, stencil, weights, profiles,
     load_sem, row_sem, send1, recv1, send2, recv2, send3, recv3, send4, recv4,
 ):
@@ -103,10 +103,17 @@
     for load in row_loads:
         load.start()
     loads = [
-        pltpu.make_async_copy(cot_hbm.at[f], cot.at[f], load_sem.at[f]) for f in range(fields)
+        [
+            pltpu.make_async_copy(
+                cot_hbm.at[f, :, pl.ds(128 * h, 128)], cot.at[f, h], load_sem.at[f, h]
+            )
+            for h in range(length // 128)
+        ]
+        for f in range(fields)
     ]
     for load in loads:
-        load.start()
+        for part in load:
+            part.start()
 
     barrier = pltpu.get_barrier_semaphore()
     for d in range(1, n):
@@ -210,13 +217,33 @@
     for o in range(n):
         sent[o, 2 * share : 2 * share + 1, :] = coeffs
 
+    row_values[0] = jnp.broadcast_to(column(low_ref, 0), (total, 128))
+    row_values[1] = jnp.broadcast_to(inverse_pivot, (total, 128))
     for f in range(fields):
-        loads[f].wait()
-        for z in range(planes):
-            line = f * planes + z
-            values = cot[f, z]
-            sent[line // share, line % share, :] = jnp.sum(values * leaves[f], axis=0)
-            sent[line // share, share + line % share, :] = jnp.sum(values * spreads[f], axis=0)
+        for load in loads[f]:
+            load.wait()
+        for h in range(length // 128):
+            at = lambda j: (f, h, pl.ds(j, planes, stride=rows), slice(None))
+            value = lambda i, j: row_values[i, f * rows + j : f * rows + j + 1, :]
+            rising = cot[at(0)]
+            scaled = [rising * value(1, 0)]
+            for j in range(1, rows):
+                rising = cot[at(j)] + value(0, j - 1) * rising
+                scaled.append(rising * value(1, j))
+            lift = value(0, rows - 1) * rising
+            adjoint = scaled[rows - 1]
+            settle[at(rows - 1)] = adjoint
+            for j in range(rows - 2, -1, -1):
+                adjoint = scaled[j] + value(0, j) * adjoint
+                settle[at(j)] = adjoint
+            lane_span = slice(128 * h, 128 * (h + 1))
+            z = 0
+            while z < planes:
+                o, up = divmod(f * planes + z, share)
+                run = min(planes - z, share - up)
+                sent[o, up : up + run, lane_span] = lift[z : z + run]
+                sent[o, share + up : share + up + run, lane_span] = adjoint[z : z + run]
+                z += run
 
     pl.semaphore_wait(barrier, n + 1)
 
@@ -225,11 +252,14 @@
         copy.start()
     got[wall] = sent[wall]
 
+    def joined(ref, f):
+        return jnp.concatenate([ref[f, h] for h in range(length // 128)], axis=1)
+
     wide_place = lax.broadcasted_iota(jnp.int32, (rows, 256), 1) % 128 // 2
     for g in range(groups):
         tile = jnp.zeros((rows, 256), jnp.float32)
         for f in range(g * pack, min(fields, (g + 1) * pack)):
-            sums = through_stencil(cot[f].reshape(planes * rows, length), weights)
+            sums = through_stencil(joined(cot, f), weights)
             for z in range(planes):
                 mine = wide_place == planes * (f % pack) + z
                 tile = jnp.where(mine, sums[z * rows : (z + 1) * rows], tile)
@@ -260,7 +290,7 @@
 
     operators = []
 
-    def settle_field(f):
+    def row_operator(f):
         span = slice(f * rows, (f + 1) * rows)
         gram = lax.dot_general(
             weighted[span], factor[span], (((0,), (0,)), ((), ())),
@@ -269,18 +299,9 @@
         high = gram.astype(jnp.bfloat16).astype(jnp.float32)
         operator = jnp.where(lane < 2 * rows, high, gram - high).astype(jnp.bfloat16)
         operators.append(operator)
-        for z in range(planes):
-            high, low = split(cot[f, z])
-            out = jnp.dot(
-                operator,
-                jnp.concatenate([high, low, high, low], axis=0),
-                preferred_element_type=jnp.float32,
-            )
-            base[f, z] = out
-            cot[f, z] = speeds[f] * out
 
     for f in range(fields):
-        settle_field(f)
+        row_operator(f)
     for d in range(1, n):
         arrive(sent, got, send1, recv1, d)
 
@@ -342,7 +363,10 @@
     narrow = lax.broadcasted_iota(jnp.int32, (rows, 128), 1)
     wide_plane = lax.broadcasted_iota(jnp.int32, (rows, 256), 1) % width // 2
     for f in range(fields):
-        slope = through_stencil(cot[f].reshape(planes * rows, length), stencil)
+        solved = joined(settle, f)
+        solved = solved.reshape(planes, rows, length)
+        flux = (solved * speeds[f]).reshape(planes * rows, length)
+        slope = through_stencil(flux, stencil)
         sums = jnp.dot(
             operators[f], stacked_both(beyond[f // pack]), preferred_element_type=jnp.float32
         )
@@ -363,7 +387,7 @@
         slope = slope + jnp.dot(
             spaced.astype(jnp.bfloat16), profiles[2], preferred_element_type=jnp.float32
         )
-        base[f] = base[f] + slope.reshape(planes, rows, length)
+        base[f] = solved + slope.reshape(planes, rows, length)
 
     for d in range(1, n):
         peer = lax.rem(wall + d, n)
@@ -450,7 +474,8 @@
         out_shape=tuple(jax.ShapeDtypeStruct(shape, f32) for shape in out_shapes),
         in_specs=[hbm] * 4,
         out_specs=(vmem,) * 4,
-        scratch_shapes=[scratch(cotangent.shape)]
+        scratch_shapes=[scratch((fields, length // 128, planes * rows, 128))] * 2
+        + [scratch((2, fields * rows, 128))]
         + [scratch(lower.shape)] * 3
         + [scratch(line_shape)] * 4
         + [scratch((end_rows, 256)), scratch((n, end_rows, 256)), scratch((n, depth, 256))]
@@ -458,7 +483,7 @@
         + [pltpu.VMEM((2, length, length), jnp.bfloat16)]
         + [pltpu.VMEM((2, length, 256), jnp.bfloat16)]
         + [pltpu.VMEM((3, 256, length), jnp.bfloat16)]
-        + [dma((fields,)), dma((3,))]
+        + [dma((fields, length // 128)), dma((3,))]
         + [dma((n,))] * 4
         + [dma((2,))] * 2
         + [dma((n,))] * 2,
@@ -467,7 +492,7 @@
         ),
     )(*[
         pltpu.with_memory_space_constraint(a, pltpu.HBM)
-        for a in (cotangent, lower, pivot, speed)
+        for a in (cotangent.reshape(fields, planes * rows, length), lower, pivot, speed)
     ])
     return pl.pallas_call(
         functools.partial(gather_kernel, fields, planes, rows, length, share),

time: 18.2 us -> 21.1 us (1.16)
  Pallas kernels: 18.1 us -> 20.9 us
    pallas_call x1, Pallas kernels: 16.4 us -> 19.3 us  [local(): pl.pallas_call(functools.partial(exchange_kernel, n, streams, fields, pla...]
where the time goes in v6:
time: 21.1 us; the launch traced here: 20.9 us
  Pallas kernels  20.9 us (99%)
    pallas_call x1, Pallas kernels, local(): pl.pallas_call(functools.partial(exchange_kernel, n, streams, fields, pla...  19.3 us
    pallas_call x1, Pallas kernels, local(): pl.pallas_call(functools.partial(gather_kernel, fields, planes, rows, len...  1.67 us

profile of v6, /device:TPU:0, one launch (start us, length us, event | category | flops | bytes accessed | tf_op | source)
XLA Modules:
  0.0 20.9 jit_solution(14819540918284656269)
XLA Ops:
  0.0 19.3 %shard_map.46 = (f32[5,16,32,256]{3,2,1,0:T(8,128)S(1)}, f32[8,24,256]{2,1,0:T(8,128)S(1)}, f32[8,24,256]{2,1,0:T(8,128)S(1)}, f32[4,5,32,128]{3,2,1,0:T(8,128)S(1)}) custom-call(f32[5,512,256]{2,1,0:T(8,128)} %bitcast.1, f32[5,32]{1,0:T(8,128)} %low_hbm.1, f32[5,32]{1,0:T(8,128)} %pivot_hbm.1, f32[5,32]{1,0:T(8,128)} %speed_hbm.1), custom_call_target="tpu_custom_call" | custom-call | tf_op jit(solution)/shard_map/pallas_call | solution.py:470
  19.3 1.7 %shard_map.47 = f32[5,16,32,256]{3,2,1,0:T(8,128)} custom-call(f32[5,16,32,256]{3,2,1,0:T(8,128)S(1)} %get-tuple-element.9.base, f32[8,24,256]{2,1,0:T(8,128)S(1)} %get-tuple-element.10.carried, f32[8,24,256]{2,1,0:T(8,128)S(1)} %get-tuple-element.11.slopes, f32[4,5,32,128]{3,2,1,0:T(8,128)S(1)} %get-tuple-element.12.columns), custom_call_target="tpu_custom_call" | custom-call | tf_op jit(solution)/shard_map/pallas_call | solution.py:497

commit v7 on v6

--- a/solution.py
+++ b/solution.py
@@ -219,31 +219,38 @@
 
     row_values[0] = jnp.broadcast_to(column(low_ref, 0), (total, 128))
     row_values[1] = jnp.broadcast_to(inverse_pivot, (total, 128))
-    for f in range(fields):
-        for load in loads[f]:
-            load.wait()
-        for h in range(length // 128):
-            at = lambda j: (f, h, pl.ds(j, planes, stride=rows), slice(None))
-            value = lambda i, j: row_values[i, f * rows + j : f * rows + j + 1, :]
-            rising = cot[at(0)]
-            scaled = [rising * value(1, 0)]
-            for j in range(1, rows):
-                rising = cot[at(j)] + value(0, j - 1) * rising
-                scaled.append(rising * value(1, j))
-            lift = value(0, rows - 1) * rising
-            adjoint = scaled[rows - 1]
-            settle[at(rows - 1)] = adjoint
-            for j in range(rows - 2, -1, -1):
-                adjoint = scaled[j] + value(0, j) * adjoint
-                settle[at(j)] = adjoint
-            lane_span = slice(128 * h, 128 * (h + 1))
-            z = 0
-            while z < planes:
-                o, up = divmod(f * planes + z, share)
-                run = min(planes - z, share - up)
-                sent[o, up : up + run, lane_span] = lift[z : z + run]
-                sent[o, share + up : share + up + run, lane_span] = adjoint[z : z + run]
-                z += run
+    for load in loads:
+        for part in load:
+            part.wait()
+    chains = [(f, h) for f in range(fields) for h in range(length // 128)]
+    at = lambda f, h, j: (f, h, pl.ds(j, planes, stride=rows), slice(None))
+    value = lambda i, f, j: row_values[i, f * rows + j : f * rows + j + 1, :]
+    rising = [cot[at(f, h, 0)] for f, h in chains]
+    scaled = [[rise * value(1, f, 0) for rise, (f, h) in zip(rising, chains)]]
+    for j in range(1, rows):
+        rising = [
+            cot[at(f, h, j)] + value(0, f, j - 1) * rise for rise, (f, h) in zip(rising, chains)
+        ]
+        scaled.append([rise * value(1, f, j) for rise, (f, h) in zip(rising, chains)])
+    lift = [value(0, f, rows - 1) * rise for rise, (f, h) in zip(rising, chains)]
+    adjoint = scaled[rows - 1]
+    for j in range(rows - 1, -1, -1):
+        if j < rows - 1:
+            adjoint = [
+                part + value(0, f, j) * below
+                for part, below, (f, h) in zip(scaled[j], adjoint, chains)
+            ]
+        for solved, (f, h) in zip(adjoint, chains):
+            settle[at(f, h, j)] = solved
+    for i, (f, h) in enumerate(chains):
+        lane_span = slice(128 * h, 128 * (h + 1))
+        z = 0
+        while z < planes:
+            o, up = divmod(f * planes + z, share)
+            run = min(planes - z, share - up)
+            sent[o, up : up + run, lane_span] = lift[i][z : z + run]
+            sent[o, share + up : share + up + run, lane_span] = adjoint[i][z : z + run]
+            z += run
 
     pl.semaphore_wait(barrier, n + 1)
 

time: 21.1 us -> 22.2 us (1.052)
  Pallas kernels: 20.9 us -> 22 us
    pallas_call x1, Pallas kernels: 19.3 us -> 20.4 us  [local(): pl.pallas_call(functools.partial(exchange_kernel, n, streams, fields, pla...]
where the time goes in v7:
time: 22.2 us; the launch traced here: 22 us
  Pallas kernels  22 us (99%)
    pallas_call x1, Pallas kernels, local(): pl.pallas_call(functools.partial(exchange_kernel, n, streams, fields, pla...  20.4 us
    pallas_call x1, Pallas kernels, local(): pl.pallas_call(functools.partial(gather_kernel, fields, planes, rows, len...  1.67 us

profile of v7, /device:TPU:0, one launch (start us, length us, event | category | flops | bytes accessed | tf_op | source)
XLA Modules:
  0.0 22.0 jit_solution(8537154312803488174)
XLA Ops:
  0.0 20.4 %shard_map.46 = (f32[5,16,32,256]{3,2,1,0:T(8,128)S(1)}, f32[8,24,256]{2,1,0:T(8,128)S(1)}, f32[8,24,256]{2,1,0:T(8,128)S(1)}, f32[4,5,32,128]{3,2,1,0:T(8,128)S(1)}) custom-call(f32[5,512,256]{2,1,0:T(8,128)} %bitcast.1, f32[5,32]{1,0:T(8,128)} %low_hbm.1, f32[5,32]{1,0:T(8,128)} %pivot_hbm.1, f32[5,32]{1,0:T(8,128)} %speed_hbm.1), custom_call_target="tpu_custom_call" | custom-call | tf_op jit(solution)/shard_map/pallas_call | solution.py:477
  20.4 1.7 %shard_map.47 = f32[5,16,32,256]{3,2,1,0:T(8,128)} custom-call(f32[5,16,32,256]{3,2,1,0:T(8,128)S(1)} %get-tuple-element.9.base, f32[8,24,256]{2,1,0:T(8,128)S(1)} %get-tuple-element.10.carried, f32[8,24,256]{2,1,0:T(8,128)S(1)} %get-tuple-element.11.slopes, f32[4,5,32,128]{3,2,1,0:T(8,128)S(1)} %get-tuple-element.12.columns), custom_call_target="tpu_custom_call" | custom-call | tf_op jit(solution)/shard_map/pallas_call | solution.py:504

commit v8 on v5

--- a/solution.py
+++ b/solution.py
@@ -279,7 +279,8 @@
             base[f, z] = out
             cot[f, z] = speeds[f] * out
 
-    for f in range(fields):
+    early = (fields + 1) // 2
+    for f in range(early):
         settle_field(f)
     for d in range(1, n):
         arrive(sent, got, send1, recv1, d)
@@ -338,6 +339,8 @@
         copy.start()
     ends_got[wall] = ends[...]
 
+    for f in range(early, fields):
+        settle_field(f)
     width = 2 * planes
     narrow = lax.broadcasted_iota(jnp.int32, (rows, 128), 1)
     wide_plane = lax.broadcasted_iota(jnp.int32, (rows, 256), 1) % width // 2

time: 18.2 us -> 18.4 us (1.011)
  no operation moved by 1% of the time
where the time goes in v8:
time: 18.4 us; the launch traced here: 18.2 us
  Pallas kernels  18.2 us (99%)
    pallas_call x1, Pallas kernels, local(): pl.pallas_call(functools.partial(exchange_kernel, n, streams, fields, pla...  16.5 us
    pallas_call x1, Pallas kernels, local(): pl.pallas_call(functools.partial(gather_kernel, fields, planes, rows, len...  1.67 us

profile of v8, /device:TPU:0, one launch (start us, length us, event | category | flops | bytes accessed | tf_op | source)
XLA Modules:
  0.0 18.2 jit_solution(1366176997223091175)
XLA Ops:
  0.0 16.5 %shard_map.46 = (f32[5,16,32,256]{3,2,1,0:T(8,128)S(1)}, f32[8,24,256]{2,1,0:T(8,128)S(1)}, f32[8,24,256]{2,1,0:T(8,128)S(1)}, f32[4,5,32,128]{3,2,1,0:T(8,128)S(1)}) custom-call(f32[5,16,32,256]{3,2,1,0:T(8,128)} %cot_hbm.1, f32[5,32]{1,0:T(8,128)} %low_hbm.1, f32[5,32]{1,0:T(8,128)} %pivot_hbm.1, f32[5,32]{1,0:T(8,128)} %speed_hbm.1), custom_call_target="tpu_custom_call" | custom-call | tf_op jit(solution)/shard_map/pallas_call | solution.py:449
  16.5 1.7 %shard_map.47 = f32[5,16,32,256]{3,2,1,0:T(8,128)} custom-call(f32[5,16,32,256]{3,2,1,0:T(8,128)S(1)} %get-tuple-element.9.base, f32[8,24,256]{2,1,0:T(8,128)S(1)} %get-tuple-element.10.carried, f32[8,24,256]{2,1,0:T(8,128)S(1)} %get-tuple-element.11.slopes, f32[4,5,32,128]{3,2,1,0:T(8,128)S(1)} %get-tuple-element.12.columns), custom_call_target="tpu_custom_call" | custom-call | tf_op jit(solution)/shard_map/pallas_call | solution.py:475
